TPU v7x, 256 devices: a whole 4x4x8 slice. The times are simulated.
256 devices in a mesh: lat: 8 (over x, core), lon: 32 (over y, z).
Axes of the slice: x: 4, y: 4, z: 8, core: 2. Of those that a mesh axis runs over, the one named last changes fastest.
Arguments:
- fields: float32 [256, 512, 320], P('lat', 'lon'), may hold values from -6 to 6
- wind_east: float32 [256, 512, 64], P('lat', 'lon'), may hold values from -0.45 to 0.45
- wind_north: float32 [256, 512, 64], P('lat', 'lon'), may hold values from -0.45 to 0.45
- owner: int32 [8, 128], P('lat', 'lon'), may hold values from 0 to 31, as said below
- counts: int32 [8, 128], P('lat', 'lon'), may hold values from 8 to 128
- w_in: bfloat16 [32, 320, 512], P('lon'), may hold values from -0.3125 to 0.3125
- w_two: bfloat16 [32, 512, 512], P('lon'), may hold values from -0.25 to 0.25
- w_three: bfloat16 [32, 512, 512], P('lon'), may hold values from -0.25 to 0.25
- w_out: bfloat16 [32, 512, 320], P('lon'), may hold values from -0.25 to 0.25
Outputs:
- updated: float32 [256, 512, 320], P('lat', 'lon')
Inputs may be any that keep to these rules, and one draw needn't show every extreme that they name: `owner`: each entry is the lon index whose scheme takes the block. Every device sends at most 1 block to any one device of its lat slab, and every device takes exactly 4 blocks.
All inputs are finite; a program needn't handle non-finite values.
Results may differ from a plain program's by a relative error of at most 0.003.
Values may be sent and summed in bfloat16 or wider, within the bound.
A program may use at most 64 MiB of HBM per device.

v0:
```python
import jax
import jax.numpy as jnp
from jax import lax
from jax.sharding import PartitionSpec as P

FIELDS = 5
COLS = 128
STEPS = 2
SWEEPS = 2


def padded_2(block, sides, width):
    for axis, dim in sides:
        count = lax.axis_size(axis)
        forward = [(i, i + 1) for i in range(count - 1)]
        forward.append((count - 1, 0))
        backward = [(target, source) for source, target in forward]
        low = lax.ppermute(
            lax.slice_in_dim(block, block.shape[dim] - width, None, axis=dim), axis, forward
        )
        high = lax.ppermute(lax.slice_in_dim(block, 0, width, axis=dim), axis, backward)
        block = jnp.concatenate([low, block, high], axis=dim)
    return block


def column_net(column, w_in, w_two, w_three, w_out):
    hidden_one = jax.nn.silu(jnp.dot(column, w_in[0], preferred_element_type=jnp.float32)).astype(
        jnp.bfloat16
    )
    hidden_two = jax.nn.silu(
        jnp.dot(hidden_one, w_two[0], preferred_element_type=jnp.float32)
    ).astype(jnp.bfloat16)
    hidden_three = jax.nn.silu(
        jnp.dot(hidden_two, w_three[0], preferred_element_type=jnp.float32)
    ).astype(jnp.bfloat16)
    return jnp.dot(hidden_three, w_out[0], preferred_element_type=jnp.float32).astype(jnp.bfloat16)


def sweep(padded, wind_pad, pad_width, first_row, total_rows):
    height = padded.shape[0]
    global_rows = first_row - pad_width + jnp.arange(height, dtype=jnp.int32)
    row_keep = ((global_rows >= 0) & (global_rows < total_rows - 1)).astype(jnp.float32)
    east_wind = 0.5 * (wind_pad[0][:, :-1] + wind_pad[0][:, 1:])
    north_wind = 0.5 * (wind_pad[1][:-1] + wind_pad[1][1:]) * row_keep[:-1, None, None]
    flux_east = (
        jnp.maximum(east_wind, 0.0) * padded[:, :-1] + jnp.minimum(east_wind, 0.0) * padded[:, 1:]
    )
    flux_north = (
        jnp.maximum(north_wind, 0.0) * padded[:-1] + jnp.minimum(north_wind, 0.0) * padded[1:]
    )
    inner_cells = padded[1:-1, 1:-1]
    return (
        inner_cells
        - (flux_east[1:-1, 1:] - flux_east[1:-1, :-1])
        - (flux_north[1:, 1:-1] - flux_north[:-1, 1:-1])
    )


def local(fields, wind_east, wind_north, owner, counts, w_in, w_two, w_three, w_out):
    row_count, col_count, feat_count = fields.shape
    lon_size = lax.axis_size("lon")
    blk_count = row_count * col_count // COLS
    slot_count = (blk_count + lon_size - 1) // lon_size
    slot_total = lon_size * slot_count
    total_rows = row_count * lax.axis_size("lat")
    first_row = lax.axis_index("lat") * row_count
    halo_width = 1
    stacked_winds = jnp.stack([wind_east, wind_north], axis=0)
    padded_winds = padded_2(stacked_winds, (("lat", 1), ("lon", 2)), halo_width)
    padded_winds = jnp.tile(padded_winds, (1, 1, 1, FIELDS))
    own_owner = owner[0]
    own_counts = counts[0]
    block_index = jnp.arange(blk_count, dtype=jnp.int32)
    same_dest = own_owner[:, None] == own_owner[None, :]
    earlier = block_index[None, :] < block_index[:, None]
    rank_slot = jnp.sum((same_dest & earlier).astype(jnp.int32), axis=1)
    slot_of = own_owner * slot_count + rank_slot
    placing = (jnp.arange(slot_total, dtype=jnp.int32)[:, None] == slot_of[None, :]).astype(
        jnp.bfloat16
    )
    live_mask = (jnp.arange(COLS, dtype=jnp.int32)[None, :] < own_counts[:, None]).astype(
        jnp.float32
    )[:, :, None]
    current = fields
    for step_index in range(STEPS):
        for sweep_index in range(SWEEPS):
            padded = padded_2(current, (("lat", 0), ("lon", 1)), 1)
            current = sweep(padded, padded_winds, 1, first_row, total_rows)
        blocks = current.astype(jnp.bfloat16).reshape(blk_count, COLS * feat_count)
        outgoing = jnp.dot(placing, blocks, preferred_element_type=jnp.float32).astype(jnp.bfloat16)
        outgoing = outgoing.reshape(lon_size, slot_count * COLS, feat_count)
        arrived = lax.all_to_all(outgoing, "lon", split_axis=0, concat_axis=0, tiled=True)
        tendency = column_net(
            arrived.reshape(slot_total * COLS, feat_count), w_in, w_two, w_three, w_out
        )
        spread = tendency.reshape(lon_size, slot_count * COLS, feat_count)
        returned = lax.all_to_all(spread, "lon", split_axis=0, concat_axis=0, tiled=True)
        home_sum = jnp.dot(
            placing.T,
            returned.reshape(slot_total, COLS * feat_count),
            preferred_element_type=jnp.float32,
        )
        added = home_sum.reshape(blk_count, COLS, feat_count) * live_mask
        current = current + added.reshape(row_count, col_count, feat_count)
    return current


def solution(mesh):
    return jax.shard_map(
        local,
        mesh=mesh,
        in_specs=(
            P("lat", "lon", None),
            P("lat", "lon", None),
            P("lat", "lon", None),
            P("lat", "lon"),
            P("lat", "lon"),
            P("lon", None, None),
            P("lon", None, None),
            P("lon", None, None),
            P("lon", None, None),
        ),
        out_specs=P("lat", "lon", None),
        check_vma=False,
    )
```

profile of v0, /device:TPU:38, one launch (start us, length us, event | category | flops | bytes accessed | tf_op | source)
XLA Modules:
  0.0 483.5 jit_solution(404271546431847712)
XLA Ops:
  10.8 6.4 %collective-permute-start.7 = (f32[34,1,320]{2,0,1:T(8,128)}, f32[34,1,320]{2,0,1:T(8,128)S(1)}, u32[]{:S(2)}, u32[]{:S(2)}) collective-permute-start(f32[34,1,320]{2,0,1:T(8,128)} %get-tuple-element.18), channel_id=1, source_target_pairs={{1,0},{2,1},{3,2},{4,3},{5,4},{6,5},{7,6},{8,7},{9,8},{10,9},{11,1... | collective-permute-start | bytes 130568 | tf_op jit(solution)/shard_map/ppermute | solution.py:21
  24.1 2.8 tile.12
  33.8 5.4 %collective-permute-start.11 = (f32[34,1,320]{2,0,1:T(8,128)S(1)}, f32[34,1,320]{2,0,1:T(8,128)S(1)}, u32[]{:S(2)}, u32[]{:S(2)}) collective-permute-start(f32[34,1,320]{2,0,1:T(8,128)S(1)} %get-tuple-element.16), channel_id=1, source_target_pairs={{1,0},{2,1},{3,2},{4,3},{5,4},{6,5},{7,6},{8,7},{9,8},{10,9},{11,1... | collective-permute-start | bytes 130568 | tf_op jit(solution)/shard_map/ppermute | solution.py:21
  41.1 4.9 %collective-permute-done.10 = f32[34,1,320]{2,0,1:T(8,128)S(1)} collective-permute-done((f32[34,1,320]{2,0,1:T(8,128)S(1)}, f32[34,1,320]{2,0,1:T(8,128)S(1)}, u32[]{:S(2)}, u32[]{:S(2)}) %collective-permute-start.10) | collective-permute-done | bytes 43552 | tf_op jit(solution)/shard_map/ppermute | solution.py:18
  50.2 3.4 convolution_convert_fusion.1
  53.6 6.2 %reshape.89 = bf16[32,128,320]{2,1,0:T(8,128)(2,1)} reshape(bf16[32,40960]{1,0:T(8,128)(2,1)} %convolution_convert_fusion.1) | data formatting | bytes 5242880 | tf_op jit(solution)/shard_map/reshape | solution.py:91
  59.9 4.5 copy.95
  64.4 73.3 %all_to_all.20 = bf16[32,128,320]{1,2,0:T(8,128)(2,1)} all-to-all(bf16[32,128,320]{1,2,0:T(8,128)(2,1)} %copy.95), channel_id=1, replica_groups=mesh['lat'=8,'lon'=32] {'lon'}, dimensions={0} | all-to-all | bytes 5242880 | tf_op jit(solution)/shard_map/all_to_all | solution.py:92
  137.7 10.6 %fusion = f32[4096,512]{1,0:T(8,128)} fusion(bf16[1,512,512]{2,1,0:T(8,128)(2,1)S(1)} %copy-done, bf16[1,320,512]{2,1,0:T(8,128)(2,1)} %param.14, bf16[32,128,320]{1,2,0:T(8,128)(2,1)} %all_to_all.20), kind=kOutput, calls=%fused_computation.10 | convolution fusion | flops 3500146688 | bytes 11862016 | tf_op jit(solution)/shard_map/dot_general | solution.py:31
  148.3 9.3 %fusion.16 = bf16[40,32,8,128]{3,2,1,0:T(8,128)(2,1)} fusion(f32[4096,512]{1,0:T(8,128)} %fusion, bf16[1,512,512]{2,1,0:T(8,128)(2,1)} %param.16, bf16[1,512,320]{1,2,0:T(8,128)(2,1)} %param.17), kind=kOutput, calls=%fused_computation.22 | convolution fusion | flops 3511943168 | bytes 11862016 | tf_op jit(solution)/shard_map/dot_general | solution.py:36
  157.6 4.0 copy.131
  161.6 5.6 %all-to-all-start.1 = ((bf16[32,128,320]{1,2,0:T(8,128)(2,1)}), bf16[32,128,320]{1,2,0:T(8,128)(2,1)}, u32[]{:S(2)}, u32[]{:S(2)}) async-start(bf16[32,128,320]{1,2,0:T(8,128)(2,1)} %bitcast.86), calls=%async_computation.1 | async-start | bytes 5242880 | tf_op jit(solution)/shard_map/all_to_all | solution.py:97
  167.3 60.5 %all-to-all-done.1 = bf16[32,128,320]{1,2,0:T(8,128)(2,1)} async-done(((bf16[32,128,320]{1,2,0:T(8,128)(2,1)}), bf16[32,128,320]{1,2,0:T(8,128)(2,1)}, u32[]{:S(2)}, u32[]{:S(2)}) %all-to-all-start.1) | async-done | bytes 2621472 | tf_op jit(solution)/shard_map/all_to_all | solution.py:97
  227.8 4.6 copy.98
  232.3 6.0 %reshape.92 = bf16[32,40960]{1,0:T(8,128)(2,1)} reshape(bf16[32,128,320]{2,1,0:T(8,128)(2,1)} %copy.98) | data formatting | bytes 5242880 | tf_op jit(solution)/shard_map/reshape | solution.py:100
  238.4 6.2 %dot_general.50 = bf16[128,320,32]{1,0,2:T(8,128)(2,1)} reshape(bf16[40960,32]{0,1:T(8,128)(2,1)} %bitcast.87) | data formatting | bytes 5242880 | tf_op jit(solution)/shard_map/dot_general | solution.py:98
  244.6 4.9 %copy.99 = bf16[128,320,32]{0,2,1:T(8,128)(2,1)} copy(bf16[128,320,32]{1,0,2:T(8,128)(2,1)} %dot_general.50) | data formatting | bytes 5242880 | tf_op jit(solution)/shard_map/dot_general | solution.py:98
  249.5 3.1 convolution_multiply_fusion.1
  259.7 3.4 collective-permute-start.15
  271.7 4.5 collective-permute-start.19
  278.1 2.5 collective-permute-done.18
  282.4 2.5 convolution_convert_fusion
  284.8 6.2 %reshape.95 = bf16[32,128,320]{2,1,0:T(8,128)(2,1)} reshape(bf16[32,40960]{1,0:T(8,128)(2,1)} %convolution_convert_fusion) | data formatting | bytes 5242880 | tf_op jit(solution)/shard_map/reshape | solution.py:91
  291.1 4.5 copy.103
  295.6 71.4 %all_to_all.21 = bf16[32,128,320]{1,2,0:T(8,128)(2,1)} all-to-all(bf16[32,128,320]{1,2,0:T(8,128)(2,1)} %copy.103), channel_id=1, replica_groups=mesh['lat'=8,'lon'=32] {'lon'}, dimensions={0} | all-to-all | bytes 5242880 | tf_op jit(solution)/shard_map/all_to_all | solution.py:92
  367.0 10.6 %fusion.2 = f32[4096,512]{1,0:T(8,128)} fusion(bf16[1,512,512]{2,1,0:T(8,128)(2,1)S(1)} %copy-done, bf16[1,320,512]{2,1,0:T(8,128)(2,1)S(1)} %copy-done.10, bf16[32,128,320]{1,2,0:T(8,128)(2,1)} %all_to_all.21), kind=kOutput, calls=%fused_computation.12 | convolution fusion | flops 3500146688 | bytes 11862016 | tf_op jit(solution)/shard_map/dot_general | solution.py:31
  377.7 9.1 %fusion.17 = bf16[40,32,8,128]{3,2,1,0:T(8,128)(2,1)} fusion(f32[4096,512]{1,0:T(8,128)} %fusion.2, bf16[1,512,512]{2,1,0:T(8,128)(2,1)S(1)} %copy-done.9, bf16[1,512,320]{1,2,0:T(8,128)(2,1)S(1)} %copy-done.11), kind=kOutput, calls=%fused_computation.23 | convolution fusion | flops 3511943168 | bytes 11862016 | tf_op jit(solution)/shard_map/dot_general | solution.py:36
  389.2 68.2 %all_to_all.22 = bf16[32,128,320]{1,2,0:T(8,128)(2,1)} all-to-all(bf16[32,128,320]{1,2,0:T(8,128)(2,1)S(1)} %bitcast.88), channel_id=1, replica_groups=mesh['lat'=8,'lon'=32] {'lon'}, dimensions={0} | all-to-all | bytes 5242880 | tf_op jit(solution)/shard_map/all_to_all | solution.py:97
  457.4 4.6 copy.106
  461.9 6.0 %reshape.98 = bf16[32,40960]{1,0:T(8,128)(2,1)} reshape(bf16[32,128,320]{2,1,0:T(8,128)(2,1)} %copy.106) | data formatting | bytes 5242880 | tf_op jit(solution)/shard_map/reshape | solution.py:100
  467.9 6.2 %dot_general.58 = bf16[128,320,32]{1,0,2:T(8,128)(2,1)} reshape(bf16[40960,32]{0,1:T(8,128)(2,1)} %bitcast.89) | data formatting | bytes 5242880 | tf_op jit(solution)/shard_map/dot_general | solution.py:98
  474.2 4.9 %copy.107 = bf16[128,320,32]{0,2,1:T(8,128)(2,1)} copy(bf16[128,320,32]{1,0,2:T(8,128)(2,1)} %dot_general.58) | data formatting | bytes 5242880 | tf_op jit(solution)/shard_map/dot_general | solution.py:98
  (113 shorter events, 56.4 us)
Async XLA Ops:
  0.0 137.7 %copy-start = (bf16[1,512,512]{2,1,0:T(8,128)(2,1)S(1)}, bf16[1,512,512]{2,1,0:T(8,128)(2,1)}, u32[]{:S(2)}) copy-start(bf16[1,512,512]{2,1,0:T(8,128)(2,1)} %param.15) | copy-start | bytes 1572868
  0.0 18.4 %copy-start.3 = (f32[32,16,64]{2,1,0:T(8,128)S(1)}, f32[32,16,64]{2,1,0:T(8,128)}, u32[]{:S(2)}) copy-start(f32[32,16,64]{2,1,0:T(8,128)} %param.11) | copy-start | bytes 393220
  0.0 18.4 %copy-start.4 = (f32[32,16,64]{2,1,0:T(8,128)S(1)}, f32[32,16,64]{2,1,0:T(8,128)}, u32[]{:S(2)}) copy-start(f32[32,16,64]{2,1,0:T(8,128)} %param.10) | copy-start | bytes 393220
  0.9 9.2 %collective-permute-start.5 = (f32[1,16,320]{2,0,1:T(1,128)S(1)}, f32[1,16,320]{2,0,1:T(1,128)S(1)}, u32[]{:S(2)}, u32[]{:S(2)}) collective-permute-start(f32[1,16,320]{2,0,1:T(1,128)S(1)} %copy.90), channel_id=1, source_target_pairs={{32,0},{64,32},{96,64},{128,96},{160,128},{192,160},{224,192},{0,2... | collective-permute-start | bytes 61448 | tf_op jit(solution)/shard_map/ppermute | solution.py:21
  1.2 8.9 %collective-permute-start.4 = (f32[1,16,320]{2,0,1:T(1,128)S(1)}, f32[1,16,320]{2,0,1:T(1,128)S(1)}, u32[]{:S(2)}, u32[]{:S(2)}) collective-permute-start(f32[1,16,320]{2,0,1:T(1,128)S(1)} %copy.89), channel_id=1, source_target_pairs={{0,32},{32,64},{64,96},{96,128},{128,160},{160,192},{192,224},{224... | collective-permute-start | bytes 61448 | tf_op jit(solution)/shard_map/ppermute | solution.py:18
  2.2 3.7 collective-permute-start.1
  3.7 3.2 collective-permute-start
  8.0 9.2 %collective-permute-start.3 = (f32[2,34,1,64]{3,2,1,0:T(1,128)S(1)}, f32[2,34,1,64]{3,2,1,0:T(1,128)S(1)}, u32[]{:S(2)}, u32[]{:S(2)}) collective-permute-start(f32[2,34,1,64]{3,2,1,0:T(1,128)S(1)} %get-tuple-element.28), channel_id=1, source_target_pairs={{1,0},{2,1},{3,2},{4,3},{5,4},{6,5},{7,6},{8,7},{9,8},{10,9},{11,1... | collective-permute-start | bytes 52232 | tf_op jit(solution)/shard_map/ppermute | solution.py:21
  8.2 10.2 %collective-permute-start.2 = (f32[2,34,1,64]{3,2,1,0:T(1,128)S(1)}, f32[2,34,1,64]{3,2,1,0:T(1,128)S(1)}, u32[]{:S(2)}, u32[]{:S(2)}) collective-permute-start(f32[2,34,1,64]{3,2,1,0:T(1,128)S(1)} %get-tuple-element.27), channel_id=1, source_target_pairs={{0,1},{1,2},{2,3},{3,4},{4,5},{5,6},{6,7},{7,8},{8,9},{9,10},{10,1... | collective-permute-start | bytes 52232 | tf_op jit(solution)/shard_map/ppermute | solution.py:18
  10.1 16.7 %copy-start.6 = (f32[1,16,320]{2,0,1:T(1,128)}, f32[1,16,320]{2,0,1:T(1,128)S(1)}, u32[]{:S(2)}) copy-start(f32[1,16,320]{2,0,1:T(1,128)S(1)} %collective-permute-done.4) | copy-start | bytes 61444
  10.8 16.0 %collective-permute-start.7 = (f32[34,1,320]{2,0,1:T(8,128)}, f32[34,1,320]{2,0,1:T(8,128)S(1)}, u32[]{:S(2)}, u32[]{:S(2)}) collective-permute-start(f32[34,1,320]{2,0,1:T(8,128)} %get-tuple-element.18), channel_id=1, source_target_pairs={{1,0},{2,1},{3,2},{4,3},{5,4},{6,5},{7,6},{8,7},{9,8},{10,9},{11,1... | collective-permute-start | bytes 130568 | tf_op jit(solution)/shard_map/ppermute | solution.py:21
  17.2 9.6 %collective-permute-start.6 = (f32[34,1,320]{2,0,1:T(8,128)S(1)}, f32[34,1,320]{2,0,1:T(8,128)S(1)}, u32[]{:S(2)}, u32[]{:S(2)}) collective-permute-start(f32[34,1,320]{2,0,1:T(8,128)S(1)} %get-tuple-element.17), channel_id=1, source_target_pairs={{0,1},{1,2},{2,3},{3,4},{4,5},{5,6},{6,7},{7,8},{8,9},{9,10},{10,1... | collective-permute-start | bytes 130568 | tf_op jit(solution)/shard_map/ppermute | solution.py:18
  27.5 1.2 copy-start.7
  28.7 1.3 copy-start.2
  30.0 1.4 copy-start.12
  30.5 1.6 collective-permute-start.9
  30.5 3.3 collective-permute-start.8
  33.8 7.3 %collective-permute-start.11 = (f32[34,1,320]{2,0,1:T(8,128)S(1)}, f32[34,1,320]{2,0,1:T(8,128)S(1)}, u32[]{:S(2)}, u32[]{:S(2)}) collective-permute-start(f32[34,1,320]{2,0,1:T(8,128)S(1)} %get-tuple-element.16), channel_id=1, source_target_pairs={{1,0},{2,1},{3,2},{4,3},{5,4},{6,5},{7,6},{8,7},{9,8},{10,9},{11,1... | collective-permute-start | bytes 130568 | tf_op jit(solution)/shard_map/ppermute | solution.py:21
  39.2 6.8 %collective-permute-start.10 = (f32[34,1,320]{2,0,1:T(8,128)S(1)}, f32[34,1,320]{2,0,1:T(8,128)S(1)}, u32[]{:S(2)}, u32[]{:S(2)}) collective-permute-start(f32[34,1,320]{2,0,1:T(8,128)S(1)} %get-tuple-element.15), channel_id=1, source_target_pairs={{0,1},{1,2},{2,3},{3,4},{4,5},{5,6},{6,7},{7,8},{8,9},{9,10},{10,1... | collective-permute-start | bytes 130568 | tf_op jit(solution)/shard_map/ppermute | solution.py:18
  161.6 5.6 %copy-start.8 = (s32[1,4]{1,0:T(1,128)S(1)}, s32[1,4]{1,0:T(1,128)}, u32[]{:S(2)}) copy-start(s32[1,4]{1,0:T(1,128)} %param.13) | copy-start | bytes 52
  161.6 66.2 %all-to-all-start.1 = ((bf16[32,128,320]{1,2,0:T(8,128)(2,1)}), bf16[32,128,320]{1,2,0:T(8,128)(2,1)}, u32[]{:S(2)}, u32[]{:S(2)}) async-start(bf16[32,128,320]{1,2,0:T(8,128)(2,1)} %bitcast.86), calls=%async_computation.1 | async-start | bytes 5242880 | tf_op jit(solution)/shard_map/all_to_all | solution.py:97
  256.4 1.5 collective-permute-start.13
  256.4 3.3 collective-permute-start.12
  259.7 5.2 %collective-permute-start.15 = (f32[34,1,320]{2,0,1:T(8,128)S(1)}, f32[34,1,320]{2,0,1:T(8,128)S(1)}, u32[]{:S(2)}, u32[]{:S(2)}) collective-permute-start(f32[34,1,320]{2,0,1:T(8,128)S(1)} %get-tuple-element.14), channel_id=1, source_target_pairs={{1,0},{2,1},{3,2},{4,3},{5,4},{6,5},{7,6},{8,7},{9,8},{10,9},{11,1... | collective-permute-start | bytes 130568 | tf_op jit(solution)/shard_map/ppermute | solution.py:21
  263.1 4.2 collective-permute-start.14
  268.4 1.5 collective-permute-start.17
  268.5 3.3 collective-permute-start.16
  271.7 6.4 %collective-permute-start.19 = (f32[34,1,320]{2,0,1:T(8,128)S(1)}, f32[34,1,320]{2,0,1:T(8,128)S(1)}, u32[]{:S(2)}, u32[]{:S(2)}) collective-permute-start(f32[34,1,320]{2,0,1:T(8,128)S(1)} %get-tuple-element.12), channel_id=1, source_target_pairs={{1,0},{2,1},{3,2},{4,3},{5,4},{6,5},{7,6},{8,7},{9,8},{10,9},{11,1... | collective-permute-start | bytes 130568 | tf_op jit(solution)/shard_map/ppermute | solution.py:21
  276.3 4.4 collective-permute-start.18
  295.6 71.4 %copy-start.10 = (bf16[1,320,512]{2,1,0:T(8,128)(2,1)S(1)}, bf16[1,320,512]{2,1,0:T(8,128)(2,1)}, u32[]{:S(2)}) copy-start(bf16[1,320,512]{2,1,0:T(8,128)(2,1)} %param.14) | copy-start | bytes 983044
  367.0 10.7 %copy-start.9 = (bf16[1,512,512]{2,1,0:T(8,128)(2,1)S(1)}, bf16[1,512,512]{2,1,0:T(8,128)(2,1)}, u32[]{:S(2)}) copy-start(bf16[1,512,512]{2,1,0:T(8,128)(2,1)} %param.16) | copy-start | bytes 1572868
  367.0 10.7 %copy-start.11 = (bf16[1,512,320]{1,2,0:T(8,128)(2,1)S(1)}, bf16[1,512,320]{1,2,0:T(8,128)(2,1)}, u32[]{:S(2)}) copy-start(bf16[1,512,320]{1,2,0:T(8,128)(2,1)} %param.17) | copy-start | bytes 983044
  (2 other events, 1.9 us)
where the time goes:
time: 492 us; the launch traced here: 484 us
  blocking collectives  213 us (43%)
  local copies, waits for them, and re-layouts  90.9 us (18%)
  waiting for transfers between devices  85.4 us (17%)
  matrix products  50.8 us (10%)
  starting transfers between devices  32.7 us (7%)
  other arithmetic  10.3 us (2%)
    all_to_all x2, blocking collectives, local(): lax.all_to_all(outgoing, 'lon', split_axis=0, concat_axis=0, tiled=True)  145 us
    all_to_all x1, blocking collectives, local(): lax.all_to_all(spread, 'lon', split_axis=0, concat_axis=0, tiled=True)  68.2 us
    all_to_all x1, waiting for transfers between devices, local(): lax.all_to_all(spread, 'lon', split_axis=0, concat_axis=0, tiled=True)  60.5 us
    dot_general x4, local copies, waits for them, and re-layouts, local(): jnp.dot(placing.T, returned.reshape(slot_total, COLS * feat_count), prefe...  22.3 us
    ppermute x10, starting transfers between devices, padded_2(): lax.ppermute(lax.slice_in_dim(block, 0, width, axis=dim), axis, backward)  21.7 us
    reshape x4, local copies, waits for them, and re-layouts, local(): outgoing = outgoing.reshape(lon_size, slot_count * COLS, feat_count)  21.6 us
    dot_general x2, matrix products, column_net(): jnp.dot(hidden_one, w_two[0], preferred_element_type=jnp.float32)  21.2 us
    dot_general x2, matrix products, column_net(): jnp.dot(hidden_three, w_out[0], preferred_element_type=jnp.float32)  18.3 us
  transfers between devices with their start and end apart: 21, of which 15 were waited for; matrix products, arithmetic and copies ran while one was open for 3% of the time, Pallas kernels for 0%

commit v1 on v0

v1 whole, which is shorter than its diff:
```python
import functools

import jax
import jax.numpy as jnp
from jax import lax
from jax.experimental import pallas as pl
from jax.experimental.pallas import tpu as pltpu
from jax.sharding import PartitionSpec as P

F32 = jnp.float32
BF16 = jnp.bfloat16
MESH = pl.DeviceIdType.MESH

STEPS = 2
COLS = 128
ROWS = 32
WIDE = 16
FEAT = 320
LEVELS = 64
HID = 512
BLKS = 4
GROUPS = 4
EXT_R = ROWS + 4
EXT_C = 24
CELLS = ROWS * WIDE
GROUP_ROWS = CELLS // GROUPS
TILES = ((0, 128), (128, 256), (256, 320))


def silu(x):
    half = 0.5 * x
    return half + half * jnp.tanh(half)


def roll(x, shift):
    return pltpu.roll(x, shift % x.shape[0], axis=0)


def kernel(
    n_lat,
    n_lon,
    fields,
    wind_east,
    wind_north,
    owner,
    counts,
    w_in,
    w_two,
    w_three,
    w_out,
    out,
    x,
    z,
    wind,
    raw_east,
    raw_north,
    coef,
    side_out,
    side_in,
    wside_out,
    wside_in,
    corner_out,
    corner_in,
    cur_bf,
    send_one,
    recv_one,
    send_two,
    recv_two,
    send_three,
    recv_three,
    send_four,
    recv_four,
    perm,
    perm_t,
    result,
    v_in,
    v_two,
    v_three,
    v_out,
    load_sem,
    halo_send,
    halo_recv,
    wind_send,
    wind_recv,
    ex_send,
    ex_recv,
    out_sem,
):
    near = n_lon // GROUPS
    piece = COLS // n_lon
    msg = BLKS * piece
    me_lat = lax.axis_index("lat")
    me = lax.axis_index("lon")
    my_group = me // near
    my_near = me % near
    north = lax.rem(me_lat + 1, n_lat)
    south = lax.rem(me_lat + n_lat - 1, n_lat)
    east = lax.rem(me + 1, n_lon)
    west = lax.rem(me + n_lon - 1, n_lon)
    corners = ((south, west), (south, east), (north, west), (north, east))

    def peer(group_step, near_step):
        group = lax.rem(my_group + group_step, GROUPS)
        return group * near + lax.rem(my_near + near_step, near)

    loads = [
        pltpu.make_async_copy(wind_east, raw_east, load_sem.at[0]),
        pltpu.make_async_copy(wind_north, raw_north, load_sem.at[1]),
        pltpu.make_async_copy(
            fields, x.at[0, pl.ds(2, ROWS), pl.ds(0, WIDE), :], load_sem.at[2]
        ),
        pltpu.make_async_copy(w_in, v_in, load_sem.at[3]),
        pltpu.make_async_copy(w_two, v_two, load_sem.at[4]),
        pltpu.make_async_copy(w_three, v_three, load_sem.at[5]),
        pltpu.make_async_copy(w_out, v_out, load_sem.at[6]),
    ]
    for load in loads:
        load.start()

    barrier = pltpu.get_barrier_semaphore()

    def greet(step, carry):
        pl.semaphore_signal(
            barrier,
            inc=1,
            device_id=(me_lat, lax.rem(me + step, n_lon)),
            device_id_type=MESH,
        )
        return carry

    lax.fori_loop(1, n_lon, greet, 0)
    for there in ((south, me), (north, me)) + corners:
        pl.semaphore_signal(barrier, inc=1, device_id=there, device_id_type=MESH)

    def clear(r, carry):
        x[0, r, pl.ds(WIDE, 8), :] = jnp.zeros((8, FEAT), F32)
        x[1, r, pl.ds(WIDE, 8), :] = jnp.zeros((8, FEAT), F32)
        wind[r, pl.ds(WIDE, 8), :] = jnp.zeros((8, 2 * LEVELS), F32)
        return carry

    lax.fori_loop(0, EXT_R, clear, 0)

    loads[0].wait()
    loads[1].wait()

    def join(r, carry):
        wind[r + 2, pl.ds(0, WIDE), :] = jnp.concatenate([raw_east[r], raw_north[r]], axis=-1)
        return carry

    lax.fori_loop(0, ROWS, join, 0)
    loads[2].wait()

    def remote(src, dst, send, recv, where):
        return pltpu.make_async_remote_copy(
            src_ref=src,
            dst_ref=dst,
            send_sem=send,
            recv_sem=recv,
            device_id=where,
            device_id_type=MESH,
        )

    def halo_copies(step):
        grid = x.at[step]
        inner = pl.ds(0, WIDE)
        copies = [
            remote(
                grid.at[pl.ds(2, 2), inner, :],
                grid.at[pl.ds(ROWS + 2, 2), inner, :],
                halo_send.at[step, 0],
                halo_recv.at[step, 0],
                (south, me),
            ),
            remote(
                grid.at[pl.ds(ROWS, 2), inner, :],
                grid.at[pl.ds(0, 2), inner, :],
                halo_send.at[step, 1],
                halo_recv.at[step, 1],
                (north, me),
            ),
        ]
        for side, there in enumerate((west, east)):
            copies.append(
                remote(
                    side_out.at[step, side],
                    side_in.at[step, side],
                    halo_send.at[step, 2 + side],
                    halo_recv.at[step, 2 + side],
                    (me_lat, there),
                )
            )
        for at, there in enumerate(corners):
            copies.append(
                remote(
                    corner_out.at[step, at],
                    corner_in.at[step, at],
                    halo_send.at[step, 4 + at],
                    halo_recv.at[step, 4 + at],
                    there,
                )
            )
        return copies

    def wind_copies():
        inner = pl.ds(0, WIDE)
        copies = [
            remote(
                wind.at[pl.ds(2, 2), inner, :],
                wind.at[pl.ds(ROWS + 2, 2), inner, :],
                wind_send.at[0],
                wind_recv.at[0],
                (south, me),
            ),
            remote(
                wind.at[pl.ds(ROWS, 2), inner, :],
                wind.at[pl.ds(0, 2), inner, :],
                wind_send.at[1],
                wind_recv.at[1],
                (north, me),
            ),
        ]
        for side, there in enumerate((west, east)):
            copies.append(
                remote(
                    wside_out.at[side],
                    wside_in.at[side],
                    wind_send.at[2 + side],
                    wind_recv.at[2 + side],
                    (me_lat, there),
                )
            )
        return copies

    corner_cells = ((2, 0), (2, WIDE - 1), (ROWS + 1, 0), (ROWS + 1, WIDE - 1))
    corner_slots = ((ROWS + 2, 16), (ROWS + 2, 23), (1, 16), (1, 23))
    side_cells = ((0, 1), (WIDE - 2, WIDE - 1))
    side_slots = ((16, 17), (22, 23))

    def stage_halo(step):
        for side in range(2):
            for at in range(2):
                side_out[step, side, at] = x[step, pl.ds(2, ROWS), side_cells[side][at], :]
        for at, (r, c) in enumerate(corner_cells):
            corner_out[step, at, pl.ds(0, 1), :] = x[step, r, pl.ds(c, 1), :]

    def place_halo(step):
        for side in range(2):
            for at in range(2):
                x[step, pl.ds(2, ROWS), side_slots[side][at], :] = side_in[step, side, at]
        for at, (r, c) in enumerate(corner_slots):
            x[step, r, pl.ds(c, 1), :] = corner_in[step, at, pl.ds(0, 1), :]

    corner_out[...] = jnp.zeros_like(corner_out)
    stage_halo(0)
    for side in range(2):
        for at in range(2):
            wside_out[side, at] = wind[pl.ds(2, ROWS), side_cells[side][at], :]
    for at, (r, c) in enumerate(corner_cells):
        corner_out[0, at, pl.ds(1, 1), pl.ds(0, 128)] = wind[r, pl.ds(c, 1), :]

    pl.semaphore_wait(barrier, n_lon - 1 + 6)

    winds = wind_copies()
    first = halo_copies(0)
    for copy in winds + first:
        copy.start()

    row_i = lax.broadcasted_iota(jnp.int32, (GROUP_ROWS, GROUP_ROWS), 0)
    col_i = lax.broadcasted_iota(jnp.int32, (GROUP_ROWS, GROUP_ROWS), 1)

    def slot_of(cell):
        blk = cell // (2 * WIDE)
        at = cell % (2 * WIDE)
        return (at // piece) * msg + blk * piece + at % piece

    shuffle = jnp.where(row_i == slot_of(col_i), 1.0, 0.0).astype(BF16)
    unshuffle = jnp.where(slot_of(row_i) == col_i, 1.0, 0.0).astype(BF16)

    for copy in winds + first:
        copy.wait_recv()
    for side in range(2):
        for at in range(2):
            wind[pl.ds(2, ROWS), side_slots[side][at], :] = wside_in[side, at]
    for at, (r, c) in enumerate(corner_slots):
        wind[r, pl.ds(c, 1), :] = corner_in[0, at, pl.ds(1, 1), pl.ds(0, 128)]
    place_halo(0)

    first_row = me_lat * ROWS
    last_face = n_lat * ROWS - 1
    low_half = lax.broadcasted_iota(jnp.int32, (EXT_C, 128), 1) < LEVELS

    def both(row):
        turned = pltpu.roll(row, LEVELS, axis=1)
        return jnp.where(low_half, row, turned), jnp.where(low_half, turned, row)

    def face_north(r, here, above):
        j = first_row + r - 2
        keep = jnp.where((j >= 0) & (j < last_face), 0.5, 0.0)
        return (here + above) * keep

    def make_coef(r, carry):
        _, n_low = both(wind[r - 1])
        e_here, n_here = both(wind[r])
        _, n_high = both(wind[r + 1])
        e_face = 0.5 * (e_here + roll(e_here, -1))
        w_face = roll(e_face, 1)
        n_face = face_north(r, n_here, n_high)
        s_face = face_north(r - 1, n_low, n_here)
        coef[0, r] = (
            1.0
            - jnp.maximum(e_face, 0.0)
            + jnp.minimum(w_face, 0.0)
            - jnp.maximum(n_face, 0.0)
            + jnp.minimum(s_face, 0.0)
        )
        coef[1, r] = -jnp.minimum(e_face, 0.0)
        coef[2, r] = jnp.maximum(w_face, 0.0)
        coef[3, r] = -jnp.minimum(n_face, 0.0)
        coef[4, r] = jnp.maximum(s_face, 0.0)
        return carry

    lax.fori_loop(1, EXT_R - 1, make_coef, 0)

    def advected(grid, r, lo, hi):
        w = hi - lo
        lanes = pl.ds(lo, w)
        first_lanes = pl.ds(0, w)
        q = grid[r, :, lanes]
        return (
            coef[0, r, :, first_lanes] * q
            + coef[1, r, :, first_lanes] * roll(q, -1)
            + coef[2, r, :, first_lanes] * roll(q, 1)
            + coef[3, r, :, first_lanes] * grid[r + 1, :, lanes]
            + coef[4, r, :, first_lanes] * grid[r - 1, :, lanes]
        )

    def owner_lanes(blk):
        return jnp.broadcast_to(owner[0, blk].astype(F32), (WIDE, 64)).astype(BF16)

    def exchange(step, phase, send, recv, group_step):
        def one(near_step, carry):
            there = peer(group_step, near_step)

            @pl.when(there != me)
            def _():
                remote(
                    send.at[step, there],
                    recv.at[step, me],
                    ex_send.at[step, phase],
                    ex_recv.at[step, phase, my_group],
                    (me_lat, there),
                ).start()

            @pl.when(there == me)
            def _():
                pltpu.make_async_copy(
                    send.at[step, me], recv.at[step, me], ex_recv.at[step, phase, my_group]
                ).start()

            return carry

        lax.fori_loop(0, near, one, 0)

    def arrived(step, phase, recv, group):
        part = recv.at[step, pl.ds(group * near, near)]
        pltpu.make_async_copy(part, part, ex_recv.at[step, phase, group]).wait()

    def group_at(group_step):
        return lax.rem(my_group + group_step, GROUPS)

    for step in range(STEPS):
        if step:
            stage_halo(step)
            copies = halo_copies(step)
            for copy in copies:
                copy.start()
            for copy in copies:
                copy.wait_recv()
            place_halo(step)

        def sweep_one(r, carry):
            for lo, hi in TILES:
                z[r, :, pl.ds(lo, hi - lo)] = advected(x.at[step], r, lo, hi)
            return carry

        lax.fori_loop(1, EXT_R - 1, sweep_one, 0)

        def sweep_two(r, carry):
            j = r - 2
            slot = (j % 8 // 2) * 8 + (j // 8) * 2 + j % 2
            for lo, hi in TILES:
                new = advected(z, r, lo, hi)[:WIDE]
                if step + 1 < STEPS:
                    x[step + 1, r, pl.ds(0, WIDE), pl.ds(lo, hi - lo)] = new
                else:
                    result[j, :, pl.ds(lo, hi - lo)] = new
                cur_bf[slot, :, pl.ds(lo, hi - lo)] = new.astype(BF16)
            if step == 0:
                cur_bf[slot, :, pl.ds(FEAT, 64)] = owner_lanes(j // 8)
            return carry

        lax.fori_loop(2, ROWS + 2, sweep_two, 0)

        def spread(group_step, carry):
            group = group_at(group_step)
            cells = cur_bf[pl.ds(group * 8, 8)].reshape(GROUP_ROWS, 384)
            moved = jnp.dot(shuffle, cells, preferred_element_type=F32).astype(BF16)
            send_one[step, pl.ds(group * near, near)] = moved.reshape(near, msg, 384)
            exchange(step, 0, send_one, recv_one, group_step)
            return carry

        lax.fori_loop(0, GROUPS, spread, 0)
        for group in range(GROUPS):
            arrived(step, 0, recv_one, group)

        if step == 0:
            lane = lax.broadcasted_iota(jnp.int32, (CELLS, 128), 1)
            tail = recv_one[0, :, :, pl.ds(256, 128)].reshape(CELLS, 128).astype(F32)
            scheme = (lane - 64).astype(F32)
            hit = jnp.where((lane >= 64) & (tail == scheme), 1.0, 0.0)
            q_i = lax.broadcasted_iota(jnp.int32, (CELLS, CELLS), 0)
            p_i = lax.broadcasted_iota(jnp.int32, (CELLS, CELLS), 1)
            before = (p_i // piece < q_i // piece) & (p_i % piece == 0)
            ahead = jnp.dot(
                jnp.where(before, 1.0, 0.0).astype(BF16),
                hit.astype(BF16),
                preferred_element_type=F32,
            )
            place = jnp.sum(hit * (scheme * msg + ahead * piece), axis=1, keepdims=True)
            part = lax.broadcasted_iota(jnp.int32, (CELLS, 1), 0) % piece
            place = place + part.astype(F32)
            picked = jnp.where(p_i.astype(F32) == place, 1.0, 0.0)
            perm_t[...] = picked.astype(BF16)
            perm[...] = picked.T.astype(BF16)

        def deliver(group_step, carry):
            group = group_at(group_step)
            rows = perm[pl.ds(group * GROUP_ROWS, GROUP_ROWS), :]
            held = recv_one[step, :, :, pl.ds(0, FEAT)].reshape(CELLS, FEAT)
            moved = jnp.dot(rows, held, preferred_element_type=F32).astype(BF16)
            send_two[step, pl.ds(group * near, near)] = moved.reshape(near, msg, FEAT)
            exchange(step, 1, send_two, recv_two, group_step)
            return carry

        lax.fori_loop(0, GROUPS, deliver, 0)

        if step == 0:
            for load in loads[3:]:
                load.wait()

        def physics(at, carry):
            group_step = lax.rem(GROUPS - at, GROUPS)
            group = group_at(group_step)
            arrived(step, 1, recv_two, group)
            column = recv_two[step, pl.ds(group * near, near)].reshape(GROUP_ROWS, FEAT)
            hidden = jnp.dot(column, v_in[0], preferred_element_type=F32)
            hidden = silu(hidden).astype(BF16)
            hidden = jnp.dot(hidden, v_two[0], preferred_element_type=F32)
            hidden = silu(hidden).astype(BF16)
            hidden = jnp.dot(hidden, v_three[0], preferred_element_type=F32)
            hidden = silu(hidden).astype(BF16)
            tendency = jnp.dot(hidden, v_out[0], preferred_element_type=F32).astype(BF16)
            send_three[step, pl.ds(group * near, near)] = tendency.reshape(near, msg, FEAT)
            exchange(step, 2, send_three, recv_three, group_step)
            return carry

        lax.fori_loop(0, GROUPS, physics, 0)
        for group in range(GROUPS):
            arrived(step, 2, recv_three, group)

        def homeward(group_step, carry):
            group = group_at(group_step)
            rows = perm_t[pl.ds(group * GROUP_ROWS, GROUP_ROWS), :]
            held = recv_three[step].reshape(CELLS, FEAT)
            moved = jnp.dot(rows, held, preferred_element_type=F32).astype(BF16)
            send_four[step, pl.ds(group * near, near)] = moved.reshape(near, msg, FEAT)
            exchange(step, 3, send_four, recv_four, group_step)
            return carry

        lax.fori_loop(0, GROUPS, homeward, 0)

        def add_home(at, carry):
            group = group_at(lax.rem(GROUPS - at, GROUPS))
            arrived(step, 3, recv_four, group)
            pieces = recv_four[step, pl.ds(group * near, near)].reshape(GROUP_ROWS, FEAT)
            home = jnp.dot(unshuffle, pieces, preferred_element_type=F32)
            for blk in range(BLKS):
                for odd in range(2):
                    j = 8 * blk + 2 * group + odd
                    lo = (2 * blk + odd) * WIDE
                    cell = (2 * group + odd) * WIDE + lax.broadcasted_iota(
                        jnp.int32, (WIDE, FEAT), 0
                    )
                    added = jnp.where(cell < counts[0, blk], home[lo : lo + WIDE], 0.0)
                    if step + 1 < STEPS:
                        x[step + 1, j + 2, pl.ds(0, WIDE), :] += added
                    else:
                        result[j] += added
            return carry

        lax.fori_loop(0, GROUPS, add_home, 0)

    finish = pltpu.make_async_copy(result, out, out_sem.at[0])
    finish.start()
    for copy in winds:
        copy.wait_send()
    for step in range(STEPS):
        for copy in halo_copies(step):
            copy.wait_send()
        for phase, send in enumerate((send_one, send_two, send_three, send_four)):
            sent = send.at[step, pl.ds(0, n_lon - 1)]
            pltpu.make_async_copy(sent, sent, ex_send.at[step, phase]).wait()
    finish.wait()


def solution(mesh):
    n_lat, n_lon = mesh.shape["lat"], mesh.shape["lon"]
    msg = BLKS * COLS // n_lon
    any_spec = pl.BlockSpec(memory_space=pl.ANY)
    smem = pl.BlockSpec(memory_space=pltpu.SMEM)
    dma = pltpu.SemaphoreType.DMA
    vmem = pltpu.VMEM
    scratch = [
        vmem((STEPS, EXT_R, EXT_C, FEAT), F32),
        vmem((EXT_R, EXT_C, FEAT), F32),
        vmem((EXT_R, EXT_C, 2 * LEVELS), F32),
        vmem((ROWS, WIDE, LEVELS), F32),
        vmem((ROWS, WIDE, LEVELS), F32),
        vmem((5, EXT_R, EXT_C, 128), F32),
        vmem((STEPS, 2, 2, ROWS, FEAT), F32),
        vmem((STEPS, 2, 2, ROWS, FEAT), F32),
        vmem((2, 2, ROWS, 128), F32),
        vmem((2, 2, ROWS, 128), F32),
        vmem((STEPS, 4, 8, FEAT), F32),
        vmem((STEPS, 4, 8, FEAT), F32),
        vmem((ROWS, WIDE, 384), BF16),
        vmem((STEPS, n_lon, msg, 384), BF16),
        vmem((STEPS, n_lon, msg, 384), BF16),
    ]
    scratch += [vmem((STEPS, n_lon, msg, FEAT), BF16)] * 6
    scratch += [
        vmem((CELLS, CELLS), BF16),
        vmem((CELLS, CELLS), BF16),
        vmem((ROWS, WIDE, FEAT), F32),
        vmem((1, FEAT, HID), BF16),
        vmem((1, HID, HID), BF16),
        vmem((1, HID, HID), BF16),
        vmem((1, HID, FEAT), BF16),
        dma((7,)),
        dma((STEPS, 8)),
        dma((STEPS, 8)),
        dma((4,)),
        dma((4,)),
        dma((STEPS, 4)),
        dma((STEPS, 4, GROUPS)),
        dma((1,)),
    ]

    call = pl.pallas_call(
        functools.partial(kernel, n_lat, n_lon),
        out_shape=jax.ShapeDtypeStruct((ROWS, WIDE, FEAT), F32),
        in_specs=[any_spec] * 3 + [smem] * 2 + [any_spec] * 4,
        out_specs=any_spec,
        scratch_shapes=scratch,
        compiler_params=pltpu.CompilerParams(
            collective_id=0, has_side_effects=True, vmem_limit_bytes=40 * 1024 * 1024
        ),
        name="coupled_steps",
    )

    return jax.shard_map(
        call,
        mesh=mesh,
        in_specs=(
            P("lat", "lon", None),
            P("lat", "lon", None),
            P("lat", "lon", None),
            P("lat", "lon"),
            P("lat", "lon"),
            P("lon", None, None),
            P("lon", None, None),
            P("lon", None, None),
            P("lon", None, None),
        ),
        out_specs=P("lat", "lon", None),
        check_vma=False,
    )
```

time: 492 us -> 128 us (0.26)
  the two profiles are of different devices: /device:TPU:38 before, /device:TPU:32 now
where the time goes in v1:
time: 128 us; the launch traced here: 127 us
  Pallas kernels  120 us (94%)
  local copies, waits for them, and re-layouts  7.17 us (6%)
    pallas_call x1, Pallas kernels  120 us
    unnamed x18, local copies, waits for them, and re-layouts  7.17 us

profile of v1, /device:TPU:32, one launch (start us, length us, event | category | flops | bytes accessed | tf_op | source)
XLA Modules:
  0.0 126.8 jit_solution(17329901019440941909)
XLA Ops:
  0.0 0.0 copy-start.1
  0.0 0.0 copy-start.7
  0.0 0.0 copy-start.6
  0.0 1.2 copy.10.w_out
  1.3 0.0 copy-done.1
  1.3 0.0 copy-done.7
  1.3 0.0 copy-done.6
  1.3 0.0 copy-start
  1.3 1.1 copy-done
  2.4 0.0 copy-start.2
  2.4 1.0 copy-done.2
  3.5 0.0 copy-start.3
  3.5 1.0 copy-done.3
  4.4 0.0 copy-start.4
  4.4 0.9 copy-done.4
  5.4 0.0 copy-start.5
  5.4 0.9 copy-done.5
  6.3 119.6 %coupled_steps.1 = f32[32,16,320]{2,1,0:T(8,128)S(1)} custom-call(f32[32,16,320]{2,1,0:T(8,128)S(1)} %copy-done, f32[32,16,64]{2,1,0:T(8,128)S(1)} %copy-done.4, f32[32,16,64]{2,1,0:T(8,128)S(1)} %copy-done.5, s32[1,4]{1,0:T(1,128)S(1)} %copy-done.6, s32[1,4]{1,0:T(1,128)S(1)} %copy-done.7, bf16[1,320,512]{2,1,0:T(8,128)(2,1)S(1)} %copy-done.3, ...), custom_call_target="tpu_custom_call" | custom-call | tf_op jit(solution)/shard_map/coupled_steps/pallas_call
  125.9 0.9 copy.12
Async XLA Ops:
  0.0 1.3 copy-start.1
  0.0 1.3 copy-start.7
  0.0 1.3 %copy-start.6 = (s32[1,4]{1,0:T(1,128)S(1)}, s32[1,4]{1,0:T(1,128)}, u32[]{:S(2)}) copy-start(s32[1,4]{1,0:T(1,128)} %owner.1) | copy-start | bytes 52
  1.3 1.1 copy-start
  2.4 1.0 copy-start.2
  3.5 1.0 copy-start.3
  4.4 0.9 copy-start.4
  5.4 0.9 copy-start.5

commit v2 on v1

--- a/solution.py
+++ b/solution.py
@@ -99,6 +99,9 @@
     west = lax.rem(me + n_lon - 1, n_lon)
     corners = ((south, west), (south, east), (north, west), (north, east))
 
+    def far_first(turn, count):
+        return lax.rem(count // 2 + (1 - 2 * (turn % 2)) * ((turn + 1) // 2) + count, count)
+
     def peer(group_step, near_step):
         group = lax.rem(my_group + group_step, GROUPS)
         return group * near + lax.rem(my_near + near_step, near)
@@ -338,8 +341,8 @@
         return jnp.broadcast_to(owner[0, blk].astype(F32), (WIDE, 64)).astype(BF16)
 
     def exchange(step, phase, send, recv, group_step):
-        def one(near_step, carry):
-            there = peer(group_step, near_step)
+        def one(turn, carry):
+            there = peer(group_step, far_first(turn, near))
 
             @pl.when(there != me)
             def _():
@@ -401,7 +404,8 @@
 
         lax.fori_loop(2, ROWS + 2, sweep_two, 0)
 
-        def spread(group_step, carry):
+        def spread(turn, carry):
+            group_step = far_first(turn, GROUPS)
             group = group_at(group_step)
             cells = cur_bf[pl.ds(group * 8, 8)].reshape(GROUP_ROWS, 384)
             moved = jnp.dot(shuffle, cells, preferred_element_type=F32).astype(BF16)
@@ -433,7 +437,8 @@
             perm_t[...] = picked.astype(BF16)
             perm[...] = picked.T.astype(BF16)
 
-        def deliver(group_step, carry):
+        def deliver(turn, carry):
+            group_step = far_first(turn, GROUPS)
             group = group_at(group_step)
             rows = perm[pl.ds(group * GROUP_ROWS, GROUP_ROWS), :]
             held = recv_one[step, :, :, pl.ds(0, FEAT)].reshape(CELLS, FEAT)
@@ -449,7 +454,7 @@
                 load.wait()
 
         def physics(at, carry):
-            group_step = lax.rem(GROUPS - at, GROUPS)
+            group_step = far_first(at, GROUPS)
             group = group_at(group_step)
             arrived(step, 1, recv_two, group)
             column = recv_two[step, pl.ds(group * near, near)].reshape(GROUP_ROWS, FEAT)
@@ -459,7 +464,9 @@
             hidden = silu(hidden).astype(BF16)
             hidden = jnp.dot(hidden, v_three[0], preferred_element_type=F32)
             hidden = silu(hidden).astype(BF16)
-            tendency = jnp.dot(hidden, v_out[0], preferred_element_type=F32).astype(BF16)
+            tendency = lax.dot_general(
+                hidden, v_out[0], (((1,), (1,)), ((), ())), preferred_element_type=F32
+            ).astype(BF16)
             send_three[step, pl.ds(group * near, near)] = tendency.reshape(near, msg, FEAT)
             exchange(step, 2, send_three, recv_three, group_step)
             return carry
@@ -468,7 +475,8 @@
         for group in range(GROUPS):
             arrived(step, 2, recv_three, group)
 
-        def homeward(group_step, carry):
+        def homeward(turn, carry):
+            group_step = far_first(turn, GROUPS)
             group = group_at(group_step)
             rows = perm_t[pl.ds(group * GROUP_ROWS, GROUP_ROWS), :]
             held = recv_three[step].reshape(CELLS, FEAT)
@@ -480,7 +488,7 @@
         lax.fori_loop(0, GROUPS, homeward, 0)
 
         def add_home(at, carry):
-            group = group_at(lax.rem(GROUPS - at, GROUPS))
+            group = group_at(far_first(at, GROUPS))
             arrived(step, 3, recv_four, group)
             pieces = recv_four[step, pl.ds(group * near, near)].reshape(GROUP_ROWS, FEAT)
             home = jnp.dot(unshuffle, pieces, preferred_element_type=F32)
@@ -545,7 +553,7 @@
         vmem((1, FEAT, HID), BF16),
         vmem((1, HID, HID), BF16),
         vmem((1, HID, HID), BF16),
-        vmem((1, HID, FEAT), BF16),
+        vmem((1, FEAT, HID), BF16),
         dma((7,)),
         dma((STEPS, 8)),
         dma((STEPS, 8)),
@@ -563,13 +571,17 @@
         out_specs=any_spec,
         scratch_shapes=scratch,
         compiler_params=pltpu.CompilerParams(
-            collective_id=0, has_side_effects=True, vmem_limit_bytes=40 * 1024 * 1024
+            collective_id=0, has_side_effects=True, vmem_limit_bytes=60 * 1024 * 1024
         ),
         name="coupled_steps",
     )
 
+    def local(fields, wind_east, wind_north, owner, counts, w_in, w_two, w_three, w_out):
+        w_out = jnp.swapaxes(w_out, 1, 2)
+        return call(fields, wind_east, wind_north, owner, counts, w_in, w_two, w_three, w_out)
+
     return jax.shard_map(
-        call,
+        local,
         mesh=mesh,
         in_specs=(
             P("lat", "lon", None),

time: 128 us -> 116 us (0.906)
  Pallas kernels: 120 us -> 113 us
  local copies, waits for them, and re-layouts: 7.17 us -> 2.06 us
    pallas_call x1, Pallas kernels: 120 us -> 113 us  [local(): call(fields, wind_east, wind_north, owner, counts, w_in, w_two, w_three,...]
    unnamed x18 -> x1, local copies, waits for them, and re-layouts: 7.17 us -> 2.06 us
where the time goes in v2:
time: 116 us; the launch traced here: 115 us
  Pallas kernels  113 us (97%)
  local copies, waits for them, and re-layouts  2.06 us (2%)
    pallas_call x1, Pallas kernels, local(): call(fields, wind_east, wind_north, owner, counts, w_in, w_two, w_three,...  113 us

profile of v2, /device:TPU:32, one launch (start us, length us, event | category | flops | bytes accessed | tf_op | source)
XLA Modules:
  0.0 114.6 jit_solution(8916322773006578624)
XLA Ops:
  0.0 112.6 %coupled_steps.1 = f32[32,16,320]{2,1,0:T(8,128)} custom-call(f32[32,16,320]{2,1,0:T(8,128)} %fields.1, f32[32,16,64]{2,1,0:T(8,128)} %wind_east.1, f32[32,16,64]{2,1,0:T(8,128)} %wind_north.1, s32[1,4]{1,0:T(1,128)} %owner.1, s32[1,4]{1,0:T(1,128)} %counts.1, bf16[1,320,512]{2,1,0:T(8,128)(2,1)} %w_in.1, bf16[1,512,512]{2,1,0:T(8,128)(2,1)} %w_two.1, ...), custom_call_target="tpu_custom_call" | custom-call | tf_op jit(solution)/shard_map/coupled_steps/pallas_call | solution.py:581
  112.6 2.1 %copy.11 = f32[32,16,320]{2,1,0:T(8,128)} copy(f32[32,16,320]{2,1,0:T(8,128)} %coupled_steps.1) | data formatting | bytes 1310720

commit v3 on v2

--- a/solution.py
+++ b/solution.py
@@ -23,8 +23,10 @@
 EXT_R = ROWS + 4
 EXT_C = 24
 CELLS = ROWS * WIDE
-GROUP_ROWS = CELLS // GROUPS
+HALF = CELLS // 2
+MAIN = 256
 TILES = ((0, 128), (128, 256), (256, 320))
+TAIL = FEAT - MAIN
 
 
 def silu(x):
@@ -70,41 +72,61 @@
     recv_three,
     send_four,
     recv_four,
+    owner_out,
+    owner_in,
     perm,
     perm_t,
+    tail_perm,
+    tail_perm_t,
     result,
     v_in,
     v_two,
     v_three,
     v_out,
+    tail_first,
+    tail_last,
     load_sem,
     halo_send,
     halo_recv,
     wind_send,
     wind_recv,
+    own_send,
+    own_recv,
     ex_send,
     ex_recv,
     out_sem,
 ):
     near = n_lon // GROUPS
+    half = near // 2
     piece = COLS // n_lon
     msg = BLKS * piece
+    pairs = msg // 2
     me_lat = lax.axis_index("lat")
     me = lax.axis_index("lon")
-    my_group = me // near
-    my_near = me % near
+    my_y = me // near
+    my_z = me % near
     north = lax.rem(me_lat + 1, n_lat)
     south = lax.rem(me_lat + n_lat - 1, n_lat)
     east = lax.rem(me + 1, n_lon)
     west = lax.rem(me + n_lon - 1, n_lon)
     corners = ((south, west), (south, east), (north, west), (north, east))
 
-    def far_first(turn, count):
-        return lax.rem(count // 2 + (1 - 2 * (turn % 2)) * ((turn + 1) // 2) + count, count)
-
-    def peer(group_step, near_step):
-        group = lax.rem(my_group + group_step, GROUPS)
-        return group * near + lax.rem(my_near + near_step, near)
+    def class_of(y, z):
+        return (y + z + me_lat) % 2
+
+    def slot_of(y, z):
+        return y * near + class_of(y, z) * half + z // 2
+
+    my_class = class_of(my_y, my_z)
+    my_slot = slot_of(my_y, my_z)
+
+    def hops(step, count):
+        return min(step, count - step)
+
+    row_order = sorted(range(GROUPS), key=lambda step: -hops(step, GROUPS))
+    all_steps = sorted(range(near), key=lambda step: -hops(step, near))
+    even_steps = [step for step in all_steps if step % 2 == 0]
+    odd_steps = [step for step in all_steps if step % 2]
 
     loads = [
         pltpu.make_async_copy(wind_east, raw_east, load_sem.at[0]),
@@ -261,6 +283,13 @@
     for at, (r, c) in enumerate(corner_cells):
         corner_out[0, at, pl.ds(1, 1), pl.ds(0, 128)] = wind[r, pl.ds(c, 1), :]
 
+    owner_row = lax.broadcasted_iota(jnp.int32, (pairs, 128), 0) % BLKS
+    owner_tile = jnp.zeros((pairs, 128), F32)
+    for blk in range(BLKS):
+        place = slot_of(owner[0, blk] // near, owner[0, blk] % near)
+        owner_tile = jnp.where(owner_row == blk, place.astype(F32), owner_tile)
+    owner_out[...] = owner_tile
+
     pl.semaphore_wait(barrier, n_lon - 1 + 6)
 
     winds = wind_copies()
@@ -268,16 +297,44 @@
     for copy in winds + first:
         copy.start()
 
-    row_i = lax.broadcasted_iota(jnp.int32, (GROUP_ROWS, GROUP_ROWS), 0)
-    col_i = lax.broadcasted_iota(jnp.int32, (GROUP_ROWS, GROUP_ROWS), 1)
-
-    def slot_of(cell):
-        blk = cell // (2 * WIDE)
-        at = cell % (2 * WIDE)
-        return (at // piece) * msg + blk * piece + at % piece
-
-    shuffle = jnp.where(row_i == slot_of(col_i), 1.0, 0.0).astype(BF16)
-    unshuffle = jnp.where(slot_of(row_i) == col_i, 1.0, 0.0).astype(BF16)
+    def tell_owner(step, carry):
+        there = lax.rem(me + step, n_lon)
+        remote(owner_out, owner_in.at[my_slot], own_send.at[0], own_recv.at[0], (me_lat, there)).start()
+        return carry
+
+    lax.fori_loop(1, n_lon, tell_owner, 0)
+    pltpu.make_async_copy(owner_out, owner_in.at[my_slot], own_recv.at[0]).start()
+
+    def iota(rows, cols):
+        return (
+            lax.broadcasted_iota(jnp.int32, (rows, cols), 0),
+            lax.broadcasted_iota(jnp.int32, (rows, cols), 1),
+        )
+
+    def one_hot(where):
+        return jnp.where(where, 1.0, 0.0).astype(BF16)
+
+    def main_row(cell):
+        blk, at = cell // (HALF // BLKS), cell % (HALF // BLKS)
+        return at // piece * msg + at % piece * BLKS + blk
+
+    def pair_row(cell):
+        blk, at = cell // (HALF // BLKS), cell % (HALF // BLKS)
+        return at // piece * pairs + at % (piece // 2) * BLKS + blk
+
+    def upper(cell):
+        return cell % piece >= piece // 2
+
+    to_i, from_i = iota(HALF, HALF)
+    shuffle = one_hot(to_i == main_row(from_i))
+    unshuffle = one_hot(main_row(to_i) == from_i)
+    to_i, from_i = iota(HALF // 2, HALF)
+    pair_low = one_hot((to_i == pair_row(from_i)) & ~upper(from_i))
+    pair_high = one_hot((to_i == pair_row(from_i)) & upper(from_i))
+    to_i, from_i = iota(HALF, HALF // 2)
+    unpair = one_hot(pair_row(to_i) == from_i)
+    is_upper = upper(to_i)
+    in_low = from_i < TAIL
 
     for copy in winds + first:
         copy.wait_recv()
@@ -337,39 +394,98 @@
             + coef[4, r, :, first_lanes] * grid[r - 1, :, lanes]
         )
 
-    def owner_lanes(blk):
-        return jnp.broadcast_to(owner[0, blk].astype(F32), (WIDE, 64)).astype(BF16)
-
-    def exchange(step, phase, send, recv, group_step):
-        def one(turn, carry):
-            there = peer(group_step, far_first(turn, near))
-
-            @pl.when(there != me)
-            def _():
-                remote(
-                    send.at[step, there],
-                    recv.at[step, me],
-                    ex_send.at[step, phase],
-                    ex_recv.at[step, phase, my_group],
-                    (me_lat, there),
-                ).start()
-
-            @pl.when(there == me)
-            def _():
-                pltpu.make_async_copy(
-                    send.at[step, me], recv.at[step, me], ex_recv.at[step, phase, my_group]
-                ).start()
-
+    def send_to(step, phase, send, recv, key, y, z, may_be_me):
+        there = slot_of(y, z)
+        arrive = ex_recv.at[step, phase, key]
+
+        def start():
+            remote(
+                send.at[step, there],
+                recv.at[step, my_slot],
+                ex_send.at[step, phase],
+                arrive,
+                (me_lat, y * near + z),
+            ).start()
+
+        if not may_be_me:
+            start()
+            return
+        pl.when(there != my_slot)(start)
+
+        @pl.when(there == my_slot)
+        def _():
+            pltpu.make_async_copy(send.at[step, there], recv.at[step, my_slot], arrive).start()
+
+    def row_at(turn):
+        step = row_order[-1]
+        for at, value in enumerate(row_order[:-1]):
+            step = jnp.where(turn == at, value, step)
+        return lax.rem(my_y + step, GROUPS)
+
+    def send_class(step, phase, send, recv, cls):
+        def one_row(turn, carry):
+            y = row_at(turn)
+            odd = (y + my_y + cls + my_class) % 2
+            for even_step, odd_step in zip(even_steps, odd_steps):
+                z = lax.rem(my_z + jnp.where(odd == 1, odd_step, even_step), near)
+                send_to(step, phase, send, recv, 0, y, z, even_step == 0)
             return carry
 
-        lax.fori_loop(0, near, one, 0)
-
-    def arrived(step, phase, recv, group):
-        part = recv.at[step, pl.ds(group * near, near)]
-        pltpu.make_async_copy(part, part, ex_recv.at[step, phase, group]).wait()
-
-    def group_at(group_step):
-        return lax.rem(my_group + group_step, GROUPS)
+        lax.fori_loop(0, GROUPS, one_row, 0)
+
+    def send_row(step, phase, send, recv, y):
+        for near_step in all_steps:
+            z = lax.rem(my_z + near_step, near)
+            send_to(step, phase, send, recv, my_class, y, z, near_step == 0)
+
+    def arrived(step, phase, recv, count, key):
+        part = recv.at[step, pl.ds(0, count)]
+        pltpu.make_async_copy(part, part, ex_recv.at[step, phase, key]).wait()
+
+    def main_of(buf, step, first, count):
+        part = buf[step, pl.ds(first, count)]
+        low = part[:, :msg].reshape(count * msg, 128)
+        high = part[:, msg : 2 * msg].reshape(count * msg, 128)
+        pair = part[:, 2 * msg :].reshape(count * pairs, 128)
+        return low, high, pair
+
+    def class_of_buf(buf, step, cls):
+        parts = [main_of(buf, step, y * near + cls * half, half) for y in range(GROUPS)]
+        low, high, pair = (jnp.concatenate(some, axis=0) for some in zip(*parts))
+        return jnp.concatenate([low, high], axis=1), pair
+
+    def put(buf, step, first, count, main, pair):
+        main, pair = main.astype(BF16), pair.astype(BF16)
+        where = pl.ds(first, count)
+        buf[step, where, pl.ds(0, msg), :] = main[:, :128].reshape(count, msg, 128)
+        buf[step, where, pl.ds(msg, msg), :] = main[:, 128:].reshape(count, msg, 128)
+        buf[step, where, pl.ds(2 * msg, pairs), :] = pair.reshape(count, pairs, 128)
+
+    def put_class(buf, step, cls, main, pair):
+        for y in range(GROUPS):
+            rows = slice(y * half * msg, (y + 1) * half * msg)
+            pair_rows = slice(y * half * pairs, (y + 1) * half * pairs)
+            put(buf, step, y * near + cls * half, half, main[rows], pair[pair_rows])
+
+    def dot(a, b):
+        return jnp.dot(a, b, preferred_element_type=F32)
+
+    def dot_t(a, b):
+        return lax.dot_general(a, b, (((1,), (1,)), ((), ())), preferred_element_type=F32)
+
+    def reorder(step, phase, held, send, recv, order, tail_order):
+        low, high, pair = main_of(held, step, 0, n_lon)
+        main = jnp.concatenate([low, high], axis=1)
+
+        def one_row(turn, carry):
+            y = row_at(turn)
+            moved = dot(order[pl.ds(y * near * msg, near * msg), :], main)
+            moved_pair = dot(tail_order[pl.ds(y * near * pairs, near * pairs), :], pair)
+            put(send, step, y * near, near, moved, moved_pair)
+            send_row(step, phase, send, recv, y)
+            return carry
+
+        lax.fori_loop(0, GROUPS, one_row, 0)
 
     for step in range(STEPS):
         if step:
@@ -390,123 +506,112 @@
 
         def sweep_two(r, carry):
             j = r - 2
-            slot = (j % 8 // 2) * 8 + (j // 8) * 2 + j % 2
+            slot = (j % 8 // 4) * 16 + (j // 8) * 4 + j % 4
             for lo, hi in TILES:
                 new = advected(z, r, lo, hi)[:WIDE]
                 if step + 1 < STEPS:
                     x[step + 1, r, pl.ds(0, WIDE), pl.ds(lo, hi - lo)] = new
                 else:
                     result[j, :, pl.ds(lo, hi - lo)] = new
-                cur_bf[slot, :, pl.ds(lo, hi - lo)] = new.astype(BF16)
-            if step == 0:
-                cur_bf[slot, :, pl.ds(FEAT, 64)] = owner_lanes(j // 8)
+                if hi == FEAT:
+                    new = jnp.concatenate([new, new], axis=1)
+                cur_bf[slot, :, pl.ds(lo, 128)] = new.astype(BF16)
             return carry
 
         lax.fori_loop(2, ROWS + 2, sweep_two, 0)
 
-        def spread(turn, carry):
-            group_step = far_first(turn, GROUPS)
-            group = group_at(group_step)
-            cells = cur_bf[pl.ds(group * 8, 8)].reshape(GROUP_ROWS, 384)
-            moved = jnp.dot(shuffle, cells, preferred_element_type=F32).astype(BF16)
-            send_one[step, pl.ds(group * near, near)] = moved.reshape(near, msg, 384)
-            exchange(step, 0, send_one, recv_one, group_step)
-            return carry
-
-        lax.fori_loop(0, GROUPS, spread, 0)
-        for group in range(GROUPS):
-            arrived(step, 0, recv_one, group)
+        for cls in range(2):
+            cells = cur_bf[pl.ds(cls * 16, 16)].reshape(HALF, 384)
+            tails = cells[:, MAIN:]
+            moved = dot(shuffle, cells[:, :MAIN])
+            moved_pair = jnp.where(in_low[: HALF // 2], dot(pair_low, tails), dot(pair_high, tails))
+            put_class(send_one, step, cls, moved, moved_pair)
+            send_class(step, 0, send_one, recv_one, cls)
 
         if step == 0:
-            lane = lax.broadcasted_iota(jnp.int32, (CELLS, 128), 1)
-            tail = recv_one[0, :, :, pl.ds(256, 128)].reshape(CELLS, 128).astype(F32)
-            scheme = (lane - 64).astype(F32)
-            hit = jnp.where((lane >= 64) & (tail == scheme), 1.0, 0.0)
-            q_i = lax.broadcasted_iota(jnp.int32, (CELLS, CELLS), 0)
-            p_i = lax.broadcasted_iota(jnp.int32, (CELLS, CELLS), 1)
-            before = (p_i // piece < q_i // piece) & (p_i % piece == 0)
-            ahead = jnp.dot(
-                jnp.where(before, 1.0, 0.0).astype(BF16),
-                hit.astype(BF16),
-                preferred_element_type=F32,
-            )
-            place = jnp.sum(hit * (scheme * msg + ahead * piece), axis=1, keepdims=True)
-            part = lax.broadcasted_iota(jnp.int32, (CELLS, 1), 0) % piece
-            place = place + part.astype(F32)
-            picked = jnp.where(p_i.astype(F32) == place, 1.0, 0.0)
+            pltpu.make_async_copy(owner_in, owner_in, own_recv.at[0]).wait()
+            count = n_lon * pairs
+            scheme = owner_in[...].reshape(count, 128)
+            lane = lax.broadcasted_iota(jnp.int32, (count, 128), 1).astype(F32)
+            hit = jnp.where(scheme == lane, 1.0, 0.0)
+            to_i, from_i = iota(count, count)
+            order_to = to_i // pairs * BLKS + to_i % BLKS
+            order_from = from_i // pairs * BLKS + from_i % BLKS
+            before = (order_from < order_to) & (from_i % pairs < BLKS)
+            ahead = dot(one_hot(before), hit.astype(BF16))
+            rank = jnp.sum(hit * ahead, axis=1, keepdims=True)
+            row = lax.broadcasted_iota(jnp.int32, (count, 1), 0) % pairs
+            inside = rank + (row // BLKS * BLKS).astype(F32)
+            tail_place = scheme[:, :1] * pairs + inside
+            picked = jnp.where(from_i.astype(F32) == tail_place, 1.0, 0.0)
+            tail_perm_t[...] = picked.astype(BF16)
+            tail_perm[...] = picked.T.astype(BF16)
+            place = (scheme[:, :1] * msg + inside).reshape(n_lon, pairs, 1)
+            place = jnp.concatenate([place, place + pairs], axis=1).reshape(n_lon * msg, 1)
+            _, from_i = iota(n_lon * msg, n_lon * msg)
+            picked = jnp.where(from_i.astype(F32) == place, 1.0, 0.0)
             perm_t[...] = picked.astype(BF16)
             perm[...] = picked.T.astype(BF16)
 
-        def deliver(turn, carry):
-            group_step = far_first(turn, GROUPS)
-            group = group_at(group_step)
-            rows = perm[pl.ds(group * GROUP_ROWS, GROUP_ROWS), :]
-            held = recv_one[step, :, :, pl.ds(0, FEAT)].reshape(CELLS, FEAT)
-            moved = jnp.dot(rows, held, preferred_element_type=F32).astype(BF16)
-            send_two[step, pl.ds(group * near, near)] = moved.reshape(near, msg, FEAT)
-            exchange(step, 1, send_two, recv_two, group_step)
-            return carry
-
-        lax.fori_loop(0, GROUPS, deliver, 0)
-
-        if step == 0:
             for load in loads[3:]:
                 load.wait()
-
-        def physics(at, carry):
-            group_step = far_first(at, GROUPS)
-            group = group_at(group_step)
-            arrived(step, 1, recv_two, group)
-            column = recv_two[step, pl.ds(group * near, near)].reshape(GROUP_ROWS, FEAT)
-            hidden = jnp.dot(column, v_in[0], preferred_element_type=F32)
-            hidden = silu(hidden).astype(BF16)
-            hidden = jnp.dot(hidden, v_two[0], preferred_element_type=F32)
-            hidden = silu(hidden).astype(BF16)
-            hidden = jnp.dot(hidden, v_three[0], preferred_element_type=F32)
-            hidden = silu(hidden).astype(BF16)
-            tendency = lax.dot_general(
-                hidden, v_out[0], (((1,), (1,)), ((), ())), preferred_element_type=F32
-            ).astype(BF16)
-            send_three[step, pl.ds(group * near, near)] = tendency.reshape(near, msg, FEAT)
-            exchange(step, 2, send_three, recv_three, group_step)
+            tail_first[...] = jnp.zeros_like(tail_first)
+            tail_last[...] = jnp.zeros_like(tail_last)
+            for at in range(2):
+                where = (pl.ds(at * TAIL, TAIL), pl.ds(at * HID, HID))
+                tail_first[where] = v_in[0, pl.ds(MAIN, TAIL), :]
+                tail_last[where] = v_out[0, pl.ds(MAIN, TAIL), :]
+
+        arrived(step, 0, recv_one, n_lon, 0)
+        reorder(step, 1, recv_one, send_two, recv_two, perm, tail_perm)
+
+        def physics(cls, carry):
+            arrived(step, 1, recv_two, n_lon // 2, cls)
+            main, pair = class_of_buf(recv_two, step, cls)
+            hidden = dot(main, v_in[0, pl.ds(0, MAIN), :])
+            extra = dot(pair, tail_first[...])
+            extra = extra.reshape(n_lon // 2, pairs, 2 * HID)
+            extra = jnp.concatenate([extra[:, :, :HID], extra[:, :, HID:]], axis=1)
+            hidden = silu(hidden + extra.reshape(HALF, HID)).astype(BF16)
+            hidden = silu(dot(hidden, v_two[0])).astype(BF16)
+            hidden = silu(dot(hidden, v_three[0]))
+            tendency = dot_t(hidden.astype(BF16), v_out[0, pl.ds(0, MAIN), :])
+            hidden = hidden.reshape(n_lon // 2, msg, HID)
+            both_cells = jnp.concatenate([hidden[:, :pairs], hidden[:, pairs:]], axis=2)
+            both_cells = both_cells.reshape(HALF // 2, 2 * HID).astype(BF16)
+            put_class(send_three, step, cls, tendency, dot_t(both_cells, tail_last[...]))
+            send_class(step, 2, send_three, recv_three, cls)
             return carry
 
-        lax.fori_loop(0, GROUPS, physics, 0)
-        for group in range(GROUPS):
-            arrived(step, 2, recv_three, group)
-
-        def homeward(turn, carry):
-            group_step = far_first(turn, GROUPS)
-            group = group_at(group_step)
-            rows = perm_t[pl.ds(group * GROUP_ROWS, GROUP_ROWS), :]
-            held = recv_three[step].reshape(CELLS, FEAT)
-            moved = jnp.dot(rows, held, preferred_element_type=F32).astype(BF16)
-            send_four[step, pl.ds(group * near, near)] = moved.reshape(near, msg, FEAT)
-            exchange(step, 3, send_four, recv_four, group_step)
+        lax.fori_loop(0, 2, physics, 0)
+
+        arrived(step, 2, recv_three, n_lon, 0)
+        reorder(step, 3, recv_three, send_four, recv_four, perm_t, tail_perm_t)
+
+        def add_home(cls, carry):
+            arrived(step, 3, recv_four, n_lon // 2, cls)
+            main, pair = class_of_buf(recv_four, step, cls)
+            home = dot(unshuffle, main)
+            tail = dot(unpair, pair)
+            tail = jnp.where(is_upper, pltpu.roll(tail, TAIL, axis=1), tail)
+            for blk in range(BLKS):
+                for r in range(4):
+                    j = 8 * blk + 4 * cls + r
+                    lo = (4 * blk + r) * WIDE
+                    first_cell = (4 * cls + r) * WIDE
+                    for at, hi in ((0, MAIN), (MAIN, FEAT)):
+                        part = home if at == 0 else tail[:, :TAIL]
+                        part = part[lo : lo + WIDE]
+                        cell = first_cell + lax.broadcasted_iota(jnp.int32, part.shape, 0)
+                        added = jnp.where(cell < counts[0, blk], part, 0.0)
+                        lanes = pl.ds(at, hi - at)
+                        if step + 1 < STEPS:
+                            x[step + 1, j + 2, pl.ds(0, WIDE), lanes] += added
+                        else:
+                            result[j, :, lanes] += added
             return carry
 
-        lax.fori_loop(0, GROUPS, homeward, 0)
-
-        def add_home(at, carry):
-            group = group_at(far_first(at, GROUPS))
-            arrived(step, 3, recv_four, group)
-            pieces = recv_four[step, pl.ds(group * near, near)].reshape(GROUP_ROWS, FEAT)
-            home = jnp.dot(unshuffle, pieces, preferred_element_type=F32)
-            for blk in range(BLKS):
-                for odd in range(2):
-                    j = 8 * blk + 2 * group + odd
-                    lo = (2 * blk + odd) * WIDE
-                    cell = (2 * group + odd) * WIDE + lax.broadcasted_iota(
-                        jnp.int32, (WIDE, FEAT), 0
-                    )
-                    added = jnp.where(cell < counts[0, blk], home[lo : lo + WIDE], 0.0)
-                    if step + 1 < STEPS:
-                        x[step + 1, j + 2, pl.ds(0, WIDE), :] += added
-                    else:
-                        result[j] += added
-            return carry
-
-        lax.fori_loop(0, GROUPS, add_home, 0)
+        lax.fori_loop(0, 2, add_home, 0)
 
     finish = pltpu.make_async_copy(result, out, out_sem.at[0])
     finish.start()
@@ -518,12 +623,15 @@
         for phase, send in enumerate((send_one, send_two, send_three, send_four)):
             sent = send.at[step, pl.ds(0, n_lon - 1)]
             pltpu.make_async_copy(sent, sent, ex_send.at[step, phase]).wait()
+    sent = owner_in.at[pl.ds(0, n_lon - 1)]
+    pltpu.make_async_copy(sent, sent, own_send.at[0]).wait()
     finish.wait()
 
 
 def solution(mesh):
     n_lat, n_lon = mesh.shape["lat"], mesh.shape["lon"]
     msg = BLKS * COLS // n_lon
+    rows = msg * FEAT // 128
     any_spec = pl.BlockSpec(memory_space=pl.ANY)
     smem = pl.BlockSpec(memory_space=pltpu.SMEM)
     dma = pltpu.SemaphoreType.DMA
@@ -542,25 +650,31 @@
         vmem((STEPS, 4, 8, FEAT), F32),
         vmem((STEPS, 4, 8, FEAT), F32),
         vmem((ROWS, WIDE, 384), BF16),
-        vmem((STEPS, n_lon, msg, 384), BF16),
-        vmem((STEPS, n_lon, msg, 384), BF16),
     ]
-    scratch += [vmem((STEPS, n_lon, msg, FEAT), BF16)] * 6
+    scratch += [vmem((STEPS, n_lon, rows, 128), BF16)] * 8
     scratch += [
+        vmem((msg // 2, 128), F32),
+        vmem((n_lon, msg // 2, 128), F32),
         vmem((CELLS, CELLS), BF16),
         vmem((CELLS, CELLS), BF16),
+        vmem((HALF, HALF), BF16),
+        vmem((HALF, HALF), BF16),
         vmem((ROWS, WIDE, FEAT), F32),
         vmem((1, FEAT, HID), BF16),
         vmem((1, HID, HID), BF16),
         vmem((1, HID, HID), BF16),
         vmem((1, FEAT, HID), BF16),
+        vmem((2 * TAIL, 2 * HID), BF16),
+        vmem((2 * TAIL, 2 * HID), BF16),
         dma((7,)),
         dma((STEPS, 8)),
         dma((STEPS, 8)),
         dma((4,)),
         dma((4,)),
+        dma((1,)),
+        dma((1,)),
         dma((STEPS, 4)),
-        dma((STEPS, 4, GROUPS)),
+        dma((STEPS, 4, 2)),
         dma((1,)),
     ]
 

time: 116 us -> 111 us (0.957)
  Pallas kernels: 113 us -> 107 us
    pallas_call x1, Pallas kernels: 113 us -> 107 us  [local(): call(fields, wind_east, wind_north, owner, counts, w_in, w_two, w_three,...]
where the time goes in v3:
time: 111 us; the launch traced here: 109 us
  Pallas kernels  107 us (96%)
  local copies, waits for them, and re-layouts  2.06 us (2%)
    pallas_call x1, Pallas kernels, local(): call(fields, wind_east, wind_north, owner, counts, w_in, w_two, w_three,...  107 us

profile of v3, /device:TPU:32, one launch (start us, length us, event | category | flops | bytes accessed | tf_op | source)
XLA Modules:
  0.0 109.3 jit_solution(8639220688905578768)
XLA Ops:
  0.0 107.2 %coupled_steps.1 = f32[32,16,320]{2,1,0:T(8,128)} custom-call(f32[32,16,320]{2,1,0:T(8,128)} %fields.1, f32[32,16,64]{2,1,0:T(8,128)} %wind_east.1, f32[32,16,64]{2,1,0:T(8,128)} %wind_north.1, s32[1,4]{1,0:T(1,128)} %owner.1, s32[1,4]{1,0:T(1,128)} %counts.1, bf16[1,320,512]{2,1,0:T(8,128)(2,1)} %w_in.1, bf16[1,512,512]{2,1,0:T(8,128)(2,1)} %w_two.1, ...), custom_call_target="tpu_custom_call" | custom-call | tf_op jit(solution)/shard_map/coupled_steps/pallas_call | solution.py:695
  107.2 2.1 %copy.11 = f32[32,16,320]{2,1,0:T(8,128)} copy(f32[32,16,320]{2,1,0:T(8,128)} %coupled_steps.1) | data formatting | bytes 1310720

commit v4 on v3

--- a/solution.py
+++ b/solution.py
@@ -27,6 +27,10 @@
 MAIN = 256
 TILES = ((0, 128), (128, 256), (256, 320))
 TAIL = FEAT - MAIN
+TWO = FEAT
+THREE = TWO + HID
+LAST = THREE + HID
+LAYERS = LAST + FEAT
 
 
 def silu(x):
@@ -79,10 +83,7 @@
     tail_perm,
     tail_perm_t,
     result,
-    v_in,
-    v_two,
-    v_three,
-    v_out,
+    weights,
     tail_first,
     tail_last,
     load_sem,
@@ -92,6 +93,8 @@
     wind_recv,
     own_send,
     own_recv,
+    share_send,
+    share_recv,
     ex_send,
     ex_recv,
     out_sem,
@@ -120,6 +123,18 @@
     my_class = class_of(my_y, my_z)
     my_slot = slot_of(my_y, my_z)
 
+    wide = near // 2
+    quarter = wide // 2
+
+    def pair_slot(y, z):
+        return y * wide + z % wide
+
+    def scheme_slot(y, z):
+        return pair_slot(y, z) * 2 + z // wide
+
+    def window_slot(y, z):
+        return y * wide + class_of(y, z) * quarter + z % wide // 2
+
     def hops(step, count):
         return min(step, count - step)
 
@@ -127,6 +142,15 @@
     all_steps = sorted(range(near), key=lambda step: -hops(step, near))
     even_steps = [step for step in all_steps if step % 2 == 0]
     odd_steps = [step for step in all_steps if step % 2]
+
+    def far_first(steps):
+        return sorted(steps, key=lambda step: (-abs(step), -step))
+
+    to_holder = [far_first(range(low, low + wide)) for low in (1 - quarter, -quarter)]
+    from_holder = [
+        [[step for step in far_first(range(low, low + wide)) if step % 2 == odd] for odd in range(2)]
+        for low in (-quarter, 1 - quarter)
+    ]
 
     loads = [
         pltpu.make_async_copy(wind_east, raw_east, load_sem.at[0]),
@@ -134,10 +158,10 @@
         pltpu.make_async_copy(
             fields, x.at[0, pl.ds(2, ROWS), pl.ds(0, WIDE), :], load_sem.at[2]
         ),
-        pltpu.make_async_copy(w_in, v_in, load_sem.at[3]),
-        pltpu.make_async_copy(w_two, v_two, load_sem.at[4]),
-        pltpu.make_async_copy(w_three, v_three, load_sem.at[5]),
-        pltpu.make_async_copy(w_out, v_out, load_sem.at[6]),
+        pltpu.make_async_copy(w_in.at[0], weights.at[0, pl.ds(0, FEAT)], load_sem.at[3]),
+        pltpu.make_async_copy(w_two.at[0], weights.at[0, pl.ds(TWO, HID)], load_sem.at[4]),
+        pltpu.make_async_copy(w_three.at[0], weights.at[0, pl.ds(THREE, HID)], load_sem.at[5]),
+        pltpu.make_async_copy(w_out.at[0], weights.at[0, pl.ds(LAST, FEAT)], load_sem.at[6]),
     ]
     for load in loads:
         load.start()
@@ -154,7 +178,18 @@
         return carry
 
     lax.fori_loop(1, n_lon, greet, 0)
-    for there in ((south, me), (north, me)) + corners:
+
+    def greet_lat(step, carry):
+        pl.semaphore_signal(
+            barrier,
+            inc=1,
+            device_id=(lax.rem(me_lat + step, n_lat), me),
+            device_id_type=MESH,
+        )
+        return carry
+
+    lax.fori_loop(1, n_lat, greet_lat, 0)
+    for there in corners:
         pl.semaphore_signal(barrier, inc=1, device_id=there, device_id_type=MESH)
 
     def clear(r, carry):
@@ -286,11 +321,11 @@
     owner_row = lax.broadcasted_iota(jnp.int32, (pairs, 128), 0) % BLKS
     owner_tile = jnp.zeros((pairs, 128), F32)
     for blk in range(BLKS):
-        place = slot_of(owner[0, blk] // near, owner[0, blk] % near)
+        place = scheme_slot(owner[0, blk] // near, owner[0, blk] % near)
         owner_tile = jnp.where(owner_row == blk, place.astype(F32), owner_tile)
     owner_out[...] = owner_tile
 
-    pl.semaphore_wait(barrier, n_lon - 1 + 6)
+    pl.semaphore_wait(barrier, n_lon - 1 + n_lat - 1 + 4)
 
     winds = wind_copies()
     first = halo_copies(0)
@@ -304,6 +339,19 @@
 
     lax.fori_loop(1, n_lon, tell_owner, 0)
     pltpu.make_async_copy(owner_out, owner_in.at[my_slot], own_recv.at[0]).start()
+
+    for load in loads[3:]:
+        load.wait()
+    other = my_y * near + lax.rem(my_z + wide, near)
+    share = LAYERS // n_lat
+
+    def share_of(which, lat):
+        return weights.at[which, pl.ds(pl.multiple_of(lat * share, 16), share)]
+
+    give = remote(
+        share_of(0, me_lat), share_of(1, me_lat), share_send.at[0], share_recv.at[0], (me_lat, other)
+    )
+    give.start()
 
     def iota(rows, cols):
         return (
@@ -395,26 +443,27 @@
         )
 
     def send_to(step, phase, send, recv, key, y, z, may_be_me):
-        there = slot_of(y, z)
+        from_slot, to_slot = (
+            (slot_of(y, z), my_slot),
+            (pair_slot(y, z), window_slot(my_y, my_z)),
+            (window_slot(y, z), pair_slot(my_y, my_z)),
+            (slot_of(y, z), my_slot),
+        )[phase]
+        there = y * near + z
         arrive = ex_recv.at[step, phase, key]
+        src, dst = send.at[step, from_slot], recv.at[step, to_slot]
 
         def start():
-            remote(
-                send.at[step, there],
-                recv.at[step, my_slot],
-                ex_send.at[step, phase],
-                arrive,
-                (me_lat, y * near + z),
-            ).start()
+            remote(src, dst, ex_send.at[step, phase], arrive, (me_lat, there)).start()
 
         if not may_be_me:
             start()
             return
-        pl.when(there != my_slot)(start)
-
-        @pl.when(there == my_slot)
+        pl.when(there != me)(start)
+
+        @pl.when(there == me)
         def _():
-            pltpu.make_async_copy(send.at[step, there], recv.at[step, my_slot], arrive).start()
+            pltpu.make_async_copy(src, dst, arrive).start()
 
     def row_at(turn):
         step = row_order[-1]
@@ -434,38 +483,53 @@
         lax.fori_loop(0, GROUPS, one_row, 0)
 
     def send_row(step, phase, send, recv, y):
-        for near_step in all_steps:
-            z = lax.rem(my_z + near_step, near)
-            send_to(step, phase, send, recv, my_class, y, z, near_step == 0)
+        if phase == 3:
+            for near_step in all_steps:
+                z = lax.rem(my_z + near_step, near)
+                send_to(step, phase, send, recv, my_class, y, z, near_step == 0)
+            return
+        for even_step, odd_step in zip(*to_holder):
+            z_step = jnp.where(my_y % 2 == 0, even_step, odd_step)
+            z = lax.rem(my_z + z_step + near, near)
+            send_to(step, phase, send, recv, my_class, y, z, 0 in (even_step, odd_step))
+
+    def send_back(step, phase, send, recv, cls):
+        def one_row(turn, carry):
+            y = row_at(turn)
+            odd = (y + my_y + cls + my_class) % 2
+            (even_even, even_odd), (odd_even, odd_odd) = from_holder
+            for steps in zip(even_even, even_odd, odd_even, odd_odd):
+                in_even = jnp.where(odd == 1, steps[1], steps[0])
+                in_odd = jnp.where(odd == 1, steps[3], steps[2])
+                z = lax.rem(my_z + jnp.where(y % 2 == 0, in_even, in_odd) + near, near)
+                send_to(step, phase, send, recv, 0, y, z, 0 in steps)
+            return carry
+
+        lax.fori_loop(0, GROUPS, one_row, 0)
 
     def arrived(step, phase, recv, count, key):
         part = recv.at[step, pl.ds(0, count)]
         pltpu.make_async_copy(part, part, ex_recv.at[step, phase, key]).wait()
 
-    def main_of(buf, step, first, count):
-        part = buf[step, pl.ds(first, count)]
-        low = part[:, :msg].reshape(count * msg, 128)
-        high = part[:, msg : 2 * msg].reshape(count * msg, 128)
-        pair = part[:, 2 * msg :].reshape(count * pairs, 128)
-        return low, high, pair
-
-    def class_of_buf(buf, step, cls):
-        parts = [main_of(buf, step, y * near + cls * half, half) for y in range(GROUPS)]
+    def main_of(buf, step, first, count, size, lo, rows):
+        where = pl.ds(first, count)
+        low = buf[step, where, pl.ds(lo, rows), :].reshape(count * rows, 128)
+        high = buf[step, where, pl.ds(size + lo, rows), :].reshape(count * rows, 128)
+        pair = buf[step, where, pl.ds(2 * size + lo // 2, rows // 2), :]
+        return low, high, pair.reshape(count * rows // 2, 128)
+
+    def joined(parts):
         low, high, pair = (jnp.concatenate(some, axis=0) for some in zip(*parts))
         return jnp.concatenate([low, high], axis=1), pair
 
-    def put(buf, step, first, count, main, pair):
+    def put(buf, step, first, count, size, lo, rows, main, pair):
         main, pair = main.astype(BF16), pair.astype(BF16)
         where = pl.ds(first, count)
-        buf[step, where, pl.ds(0, msg), :] = main[:, :128].reshape(count, msg, 128)
-        buf[step, where, pl.ds(msg, msg), :] = main[:, 128:].reshape(count, msg, 128)
-        buf[step, where, pl.ds(2 * msg, pairs), :] = pair.reshape(count, pairs, 128)
-
-    def put_class(buf, step, cls, main, pair):
-        for y in range(GROUPS):
-            rows = slice(y * half * msg, (y + 1) * half * msg)
-            pair_rows = slice(y * half * pairs, (y + 1) * half * pairs)
-            put(buf, step, y * near + cls * half, half, main[rows], pair[pair_rows])
+        buf[step, where, pl.ds(lo, rows), :] = main[:, :128].reshape(count, rows, 128)
+        buf[step, where, pl.ds(size + lo, rows), :] = main[:, 128:].reshape(count, rows, 128)
+        buf[step, where, pl.ds(2 * size + lo // 2, rows // 2), :] = pair.reshape(
+            count, rows // 2, 128
+        )
 
     def dot(a, b):
         return jnp.dot(a, b, preferred_element_type=F32)
@@ -473,15 +537,15 @@
     def dot_t(a, b):
         return lax.dot_general(a, b, (((1,), (1,)), ((), ())), preferred_element_type=F32)
 
-    def reorder(step, phase, held, send, recv, order, tail_order):
-        low, high, pair = main_of(held, step, 0, n_lon)
-        main = jnp.concatenate([low, high], axis=1)
+    def reorder(step, phase, held, held_count, held_size, send, recv, size, order, tail_order):
+        main, pair = joined([main_of(held, step, 0, held_count, held_size, 0, held_size)])
+        count = near * msg // size
 
         def one_row(turn, carry):
             y = row_at(turn)
             moved = dot(order[pl.ds(y * near * msg, near * msg), :], main)
             moved_pair = dot(tail_order[pl.ds(y * near * pairs, near * pairs), :], pair)
-            put(send, step, y * near, near, moved, moved_pair)
+            put(send, step, y * count, count, size, 0, size, moved, moved_pair)
             send_row(step, phase, send, recv, y)
             return carry
 
@@ -525,10 +589,24 @@
             tails = cells[:, MAIN:]
             moved = dot(shuffle, cells[:, :MAIN])
             moved_pair = jnp.where(in_low[: HALF // 2], dot(pair_low, tails), dot(pair_high, tails))
-            put_class(send_one, step, cls, moved, moved_pair)
+            for y in range(GROUPS):
+                rows = slice(y * half * msg, (y + 1) * half * msg)
+                pair_rows = slice(y * half * pairs, (y + 1) * half * pairs)
+                first = y * near + cls * half
+                put(send_one, step, first, half, msg, 0, msg, moved[rows], moved_pair[pair_rows])
             send_class(step, 0, send_one, recv_one, cls)
 
         if step == 0:
+            give.wait_recv()
+
+            def hand_on(at, carry):
+                lat = lax.rem(me_lat + at, n_lat)
+                mine = share_of(1, me_lat)
+                remote(mine, mine, share_send.at[1], share_recv.at[1], (lat, me)).start()
+                return carry
+
+            lax.fori_loop(1, n_lat, hand_on, 0)
+
             pltpu.make_async_copy(owner_in, owner_in, own_recv.at[0]).wait()
             count = n_lon * pairs
             scheme = owner_in[...].reshape(count, 128)
@@ -553,44 +631,64 @@
             perm_t[...] = picked.astype(BF16)
             perm[...] = picked.T.astype(BF16)
 
-            for load in loads[3:]:
-                load.wait()
+        arrived(step, 0, recv_one, n_lon, 0)
+        reorder(
+            step, 1, recv_one, n_lon, msg, send_two, recv_two, 2 * msg, perm, tail_perm
+        )
+
+        if step == 0:
+            handed = weights.at[1, pl.ds(0, LAYERS - share)]
+            pltpu.make_async_copy(handed, handed, share_recv.at[1]).wait()
             tail_first[...] = jnp.zeros_like(tail_first)
             tail_last[...] = jnp.zeros_like(tail_last)
-            for at in range(2):
-                where = (pl.ds(at * TAIL, TAIL), pl.ds(at * HID, HID))
-                tail_first[where] = v_in[0, pl.ds(MAIN, TAIL), :]
-                tail_last[where] = v_out[0, pl.ds(MAIN, TAIL), :]
-
-        arrived(step, 0, recv_one, n_lon, 0)
-        reorder(step, 1, recv_one, send_two, recv_two, perm, tail_perm)
+            for which in range(2):
+                for at in range(2):
+                    rows, lanes = pl.ds(at * TAIL, TAIL), pl.ds(at * HID, HID)
+                    tail_first[which, rows, lanes] = weights[which, pl.ds(MAIN, TAIL), :]
+                    tail_last[which, rows, lanes] = weights[which, pl.ds(LAST + MAIN, TAIL), :]
 
         def physics(cls, carry):
-            arrived(step, 1, recv_two, n_lon // 2, cls)
-            main, pair = class_of_buf(recv_two, step, cls)
-            hidden = dot(main, v_in[0, pl.ds(0, MAIN), :])
-            extra = dot(pair, tail_first[...])
-            extra = extra.reshape(n_lon // 2, pairs, 2 * HID)
-            extra = jnp.concatenate([extra[:, :, :HID], extra[:, :, HID:]], axis=1)
-            hidden = silu(hidden + extra.reshape(HALF, HID)).astype(BF16)
-            hidden = silu(dot(hidden, v_two[0])).astype(BF16)
-            hidden = silu(dot(hidden, v_three[0]))
-            tendency = dot_t(hidden.astype(BF16), v_out[0, pl.ds(0, MAIN), :])
-            hidden = hidden.reshape(n_lon // 2, msg, HID)
-            both_cells = jnp.concatenate([hidden[:, :pairs], hidden[:, pairs:]], axis=2)
-            both_cells = both_cells.reshape(HALF // 2, 2 * HID).astype(BF16)
-            put_class(send_three, step, cls, tendency, dot_t(both_cells, tail_last[...]))
-            send_class(step, 2, send_three, recv_three, cls)
+            arrived(step, 1, recv_two, n_lon // 4, cls)
+            messages = n_lon // 4
+            for scheme in range(2):
+                which = (scheme + my_z // wide) % 2
+                places = [y * wide + cls * quarter for y in range(GROUPS)]
+                part = (quarter, 2 * msg, scheme * msg, msg)
+                main, pair = joined([main_of(recv_two, step, first, *part) for first in places])
+                hidden = dot(main, weights[which, pl.ds(0, MAIN), :])
+                extra = dot(pair, tail_first[which])
+                extra = extra.reshape(messages, pairs, 2 * HID)
+                extra = jnp.concatenate([extra[:, :, :HID], extra[:, :, HID:]], axis=1)
+                hidden = silu(hidden + extra.reshape(messages * msg, HID)).astype(BF16)
+                hidden = silu(dot(hidden, weights[which, pl.ds(TWO, HID), :])).astype(BF16)
+                hidden = silu(dot(hidden, weights[which, pl.ds(THREE, HID), :]))
+                tendency = dot_t(hidden.astype(BF16), weights[which, pl.ds(LAST, MAIN), :])
+                hidden = hidden.reshape(messages, msg, HID)
+                both_cells = jnp.concatenate([hidden[:, :pairs], hidden[:, pairs:]], axis=2)
+                both_cells = both_cells.reshape(messages * pairs, 2 * HID).astype(BF16)
+                tail = dot_t(both_cells, tail_last[which])
+                for y, first in enumerate(places):
+                    rows = slice(y * quarter * msg, (y + 1) * quarter * msg)
+                    pair_rows = slice(y * quarter * pairs, (y + 1) * quarter * pairs)
+                    put(send_three, step, first, *part, tendency[rows], tail[pair_rows])
+            send_back(step, 2, send_three, recv_three, cls)
             return carry
 
         lax.fori_loop(0, 2, physics, 0)
 
-        arrived(step, 2, recv_three, n_lon, 0)
-        reorder(step, 3, recv_three, send_four, recv_four, perm_t, tail_perm_t)
+        arrived(step, 2, recv_three, n_lon // 2, 0)
+        reorder(
+            step, 3, recv_three, n_lon // 2, 2 * msg, send_four, recv_four, msg, perm_t, tail_perm_t
+        )
 
         def add_home(cls, carry):
             arrived(step, 3, recv_four, n_lon // 2, cls)
-            main, pair = class_of_buf(recv_four, step, cls)
+            main, pair = joined(
+                [
+                    main_of(recv_four, step, y * near + cls * half, half, msg, 0, msg)
+                    for y in range(GROUPS)
+                ]
+            )
             home = dot(unshuffle, main)
             tail = dot(unpair, pair)
             tail = jnp.where(is_upper, pltpu.roll(tail, TAIL, axis=1), tail)
@@ -621,10 +719,13 @@
         for copy in halo_copies(step):
             copy.wait_send()
         for phase, send in enumerate((send_one, send_two, send_three, send_four)):
-            sent = send.at[step, pl.ds(0, n_lon - 1)]
+            sent = send.at[step, pl.ds(0, send.shape[1] - 1)]
             pltpu.make_async_copy(sent, sent, ex_send.at[step, phase]).wait()
     sent = owner_in.at[pl.ds(0, n_lon - 1)]
     pltpu.make_async_copy(sent, sent, own_send.at[0]).wait()
+    give.wait_send()
+    sent = weights.at[1, pl.ds(0, LAYERS - share)]
+    pltpu.make_async_copy(sent, sent, share_send.at[1]).wait()
     finish.wait()
 
 
@@ -651,7 +752,9 @@
         vmem((STEPS, 4, 8, FEAT), F32),
         vmem((ROWS, WIDE, 384), BF16),
     ]
-    scratch += [vmem((STEPS, n_lon, rows, 128), BF16)] * 8
+    whole = vmem((STEPS, n_lon, rows, 128), BF16)
+    paired = vmem((STEPS, n_lon // 2, 2 * rows, 128), BF16)
+    scratch += [whole, whole, paired, paired, paired, paired, whole, whole]
     scratch += [
         vmem((msg // 2, 128), F32),
         vmem((n_lon, msg // 2, 128), F32),
@@ -660,12 +763,9 @@
         vmem((HALF, HALF), BF16),
         vmem((HALF, HALF), BF16),
         vmem((ROWS, WIDE, FEAT), F32),
-        vmem((1, FEAT, HID), BF16),
-        vmem((1, HID, HID), BF16),
-        vmem((1, HID, HID), BF16),
-        vmem((1, FEAT, HID), BF16),
-        vmem((2 * TAIL, 2 * HID), BF16),
-        vmem((2 * TAIL, 2 * HID), BF16),
+        vmem((2, LAYERS, HID), BF16),
+        vmem((2, 2 * TAIL, 2 * HID), BF16),
+        vmem((2, 2 * TAIL, 2 * HID), BF16),
         dma((7,)),
         dma((STEPS, 8)),
         dma((STEPS, 8)),
@@ -673,6 +773,8 @@
         dma((4,)),
         dma((1,)),
         dma((1,)),
+        dma((2,)),
+        dma((2,)),
         dma((STEPS, 4)),
         dma((STEPS, 4, 2)),
         dma((1,)),

time: 111 us -> 113 us (1.018)
  Pallas kernels: 107 us -> 110 us
    pallas_call x1, Pallas kernels: 107 us -> 110 us  [local(): call(fields, wind_east, wind_north, owner, counts, w_in, w_two, w_three,...]
where the time goes in v4:
time: 113 us; the launch traced here: 112 us
  Pallas kernels  110 us (97%)
  local copies, waits for them, and re-layouts  2.06 us (2%)
    pallas_call x1, Pallas kernels, local(): call(fields, wind_east, wind_north, owner, counts, w_in, w_two, w_three,...  110 us

profile of v4, /device:TPU:32, one launch (start us, length us, event | category | flops | bytes accessed | tf_op | source)
XLA Modules:
  0.0 111.7 jit_solution(17983991424001008779)
XLA Ops:
  0.0 109.6 %coupled_steps.1 = f32[32,16,320]{2,1,0:T(8,128)} custom-call(f32[32,16,320]{2,1,0:T(8,128)} %fields.1, f32[32,16,64]{2,1,0:T(8,128)} %wind_east.1, f32[32,16,64]{2,1,0:T(8,128)} %wind_north.1, s32[1,4]{1,0:T(1,128)} %owner.1, s32[1,4]{1,0:T(1,128)} %counts.1, bf16[1,320,512]{2,1,0:T(8,128)(2,1)} %w_in.1, bf16[1,512,512]{2,1,0:T(8,128)(2,1)} %w_two.1, ...), custom_call_target="tpu_custom_call" | custom-call | tf_op jit(solution)/shard_map/coupled_steps/pallas_call | solution.py:797
  109.6 2.1 %copy.11 = f32[32,16,320]{2,1,0:T(8,128)} copy(f32[32,16,320]{2,1,0:T(8,128)} %coupled_steps.1) | data formatting | bytes 1310720

commit v5 on v3

--- a/solution.py
+++ b/solution.py
@@ -261,17 +261,37 @@
     side_cells = ((0, 1), (WIDE - 2, WIDE - 1))
     side_slots = ((16, 17), (22, 23))
 
+    def iota(rows, cols):
+        return (
+            lax.broadcasted_iota(jnp.int32, (rows, cols), 0),
+            lax.broadcasted_iota(jnp.int32, (rows, cols), 1),
+        )
+
+    def one_hot(where):
+        return jnp.where(where, 1.0, 0.0).astype(BF16)
+
+    def dot(a, b):
+        return jnp.dot(a, b, preferred_element_type=F32)
+
+    to_i, from_i = iota(4 * ROWS, CELLS)
+    side, second = to_i // (2 * ROWS), to_i // ROWS % 2
+    pick_sides = one_hot(from_i == to_i % ROWS * WIDE + side * (WIDE - 2) + second)
+    to_i, from_i = iota(8 * ROWS, 4 * ROWS)
+    side, second = from_i // (2 * ROWS), from_i // ROWS % 2
+    place_sides = one_hot(
+        (to_i // 8 == from_i % ROWS) & (to_i % 8 == side * (EXT_C - WIDE - 2) + second)
+    )
+
     def stage_halo(step):
-        for side in range(2):
-            for at in range(2):
-                side_out[step, side, at] = x[step, pl.ds(2, ROWS), side_cells[side][at], :]
+        cells = x[step, pl.ds(2, ROWS), pl.ds(0, WIDE), :].astype(BF16).reshape(CELLS, FEAT)
+        picked = dot(pick_sides, cells).astype(BF16)
+        side_out[step] = picked.reshape(2, 2 * ROWS, FEAT)
         for at, (r, c) in enumerate(corner_cells):
             corner_out[step, at, pl.ds(0, 1), :] = x[step, r, pl.ds(c, 1), :]
 
     def place_halo(step):
-        for side in range(2):
-            for at in range(2):
-                x[step, pl.ds(2, ROWS), side_slots[side][at], :] = side_in[step, side, at]
+        sides = dot(place_sides, side_in[step].reshape(4 * ROWS, FEAT))
+        x[step, pl.ds(2, ROWS), pl.ds(WIDE, 8), :] = sides.reshape(ROWS, 8, FEAT)
         for at, (r, c) in enumerate(corner_slots):
             x[step, r, pl.ds(c, 1), :] = corner_in[step, at, pl.ds(0, 1), :]
 
@@ -304,15 +324,6 @@
 
     lax.fori_loop(1, n_lon, tell_owner, 0)
     pltpu.make_async_copy(owner_out, owner_in.at[my_slot], own_recv.at[0]).start()
-
-    def iota(rows, cols):
-        return (
-            lax.broadcasted_iota(jnp.int32, (rows, cols), 0),
-            lax.broadcasted_iota(jnp.int32, (rows, cols), 1),
-        )
-
-    def one_hot(where):
-        return jnp.where(where, 1.0, 0.0).astype(BF16)
 
     def main_row(cell):
         blk, at = cell // (HALF // BLKS), cell % (HALF // BLKS)
@@ -359,40 +370,41 @@
         return (here + above) * keep
 
     def make_coef(r, carry):
-        _, n_low = both(wind[r - 1])
-        e_here, n_here = both(wind[r])
-        _, n_high = both(wind[r + 1])
+        e_here, n_here, s_face = carry
+        e_high, n_high = both(wind[r + 1])
         e_face = 0.5 * (e_here + roll(e_here, -1))
         w_face = roll(e_face, 1)
         n_face = face_north(r, n_here, n_high)
-        s_face = face_north(r - 1, n_low, n_here)
-        coef[0, r] = (
-            1.0
-            - jnp.maximum(e_face, 0.0)
-            + jnp.minimum(w_face, 0.0)
-            - jnp.maximum(n_face, 0.0)
-            + jnp.minimum(s_face, 0.0)
-        )
-        coef[1, r] = -jnp.minimum(e_face, 0.0)
-        coef[2, r] = jnp.maximum(w_face, 0.0)
-        coef[3, r] = -jnp.minimum(n_face, 0.0)
-        coef[4, r] = jnp.maximum(s_face, 0.0)
-        return carry
-
-    lax.fori_loop(1, EXT_R - 1, make_coef, 0)
-
-    def advected(grid, r, lo, hi):
-        w = hi - lo
-        lanes = pl.ds(lo, w)
-        first_lanes = pl.ds(0, w)
-        q = grid[r, :, lanes]
-        return (
-            coef[0, r, :, first_lanes] * q
-            + coef[1, r, :, first_lanes] * roll(q, -1)
-            + coef[2, r, :, first_lanes] * roll(q, 1)
-            + coef[3, r, :, first_lanes] * grid[r + 1, :, lanes]
-            + coef[4, r, :, first_lanes] * grid[r - 1, :, lanes]
-        )
+        e_neg, w_pos = jnp.minimum(e_face, 0.0), jnp.maximum(w_face, 0.0)
+        n_neg, s_pos = jnp.minimum(n_face, 0.0), jnp.maximum(s_face, 0.0)
+        coef[0, r] = 1.0 - (e_face - e_neg) + (w_face - w_pos) - (n_face - n_neg) + (s_face - s_pos)
+        coef[1, r] = -e_neg
+        coef[2, r] = w_pos
+        coef[3, r] = -n_neg
+        coef[4, r] = s_pos
+        return e_high, n_high, n_face
+
+    _, n_first = both(wind[0])
+    e_second, n_second = both(wind[1])
+    below = face_north(0, n_first, n_second)
+    lax.fori_loop(1, EXT_R - 1, make_coef, (e_second, n_second, below), unroll=2)
+
+    def advected(grid, r, cols):
+        at = pl.ds(0, cols)
+        here, east_of, west_of, north_of, south_of = (coef[k, r, at, :] for k in range(5))
+        out_tiles = []
+        for lo, hi in TILES:
+            lanes = pl.ds(lo, hi - lo)
+            keep = slice(0, hi - lo)
+            q = grid[r, :, lanes]
+            out_tiles.append(
+                here[:, keep] * q[:cols]
+                + east_of[:, keep] * roll(q, -1)[:cols]
+                + west_of[:, keep] * roll(q, 1)[:cols]
+                + north_of[:, keep] * grid[r + 1, at, lanes]
+                + south_of[:, keep] * grid[r - 1, at, lanes]
+            )
+        return out_tiles
 
     def send_to(step, phase, send, recv, key, y, z, may_be_me):
         there = slot_of(y, z)
@@ -466,9 +478,6 @@
             rows = slice(y * half * msg, (y + 1) * half * msg)
             pair_rows = slice(y * half * pairs, (y + 1) * half * pairs)
             put(buf, step, y * near + cls * half, half, main[rows], pair[pair_rows])
-
-    def dot(a, b):
-        return jnp.dot(a, b, preferred_element_type=F32)
 
     def dot_t(a, b):
         return lax.dot_general(a, b, (((1,), (1,)), ((), ())), preferred_element_type=F32)
@@ -498,17 +507,16 @@
             place_halo(step)
 
         def sweep_one(r, carry):
-            for lo, hi in TILES:
-                z[r, :, pl.ds(lo, hi - lo)] = advected(x.at[step], r, lo, hi)
+            for (lo, hi), new in zip(TILES, advected(x.at[step], r, EXT_C)):
+                z[r, :, pl.ds(lo, hi - lo)] = new
             return carry
 
-        lax.fori_loop(1, EXT_R - 1, sweep_one, 0)
+        lax.fori_loop(1, EXT_R - 1, sweep_one, 0, unroll=2)
 
         def sweep_two(r, carry):
             j = r - 2
             slot = (j % 8 // 4) * 16 + (j // 8) * 4 + j % 4
-            for lo, hi in TILES:
-                new = advected(z, r, lo, hi)[:WIDE]
+            for (lo, hi), new in zip(TILES, advected(z, r, WIDE)):
                 if step + 1 < STEPS:
                     x[step + 1, r, pl.ds(0, WIDE), pl.ds(lo, hi - lo)] = new
                 else:
@@ -518,7 +526,7 @@
                 cur_bf[slot, :, pl.ds(lo, 128)] = new.astype(BF16)
             return carry
 
-        lax.fori_loop(2, ROWS + 2, sweep_two, 0)
+        lax.fori_loop(2, ROWS + 2, sweep_two, 0, unroll=2)
 
         for cls in range(2):
             cells = cur_bf[pl.ds(cls * 16, 16)].reshape(HALF, 384)
@@ -643,8 +651,8 @@
         vmem((ROWS, WIDE, LEVELS), F32),
         vmem((ROWS, WIDE, LEVELS), F32),
         vmem((5, EXT_R, EXT_C, 128), F32),
-        vmem((STEPS, 2, 2, ROWS, FEAT), F32),
-        vmem((STEPS, 2, 2, ROWS, FEAT), F32),
+        vmem((STEPS, 2, 2 * ROWS, FEAT), BF16),
+        vmem((STEPS, 2, 2 * ROWS, FEAT), BF16),
         vmem((2, 2, ROWS, 128), F32),
         vmem((2, 2, ROWS, 128), F32),
         vmem((STEPS, 4, 8, FEAT), F32),

time: 111 us -> 104 us (0.937); the launches traced: 109 us -> 104 us
  Pallas kernels: 107 us -> 102 us
    pallas_call x1, Pallas kernels: 107 us -> 102 us  [local(): call(fields, wind_east, wind_north, owner, counts, w_in, w_two, w_three,...]
where the time goes in v5:
time: 104 us
  Pallas kernels  102 us (98%)
  local copies, waits for them, and re-layouts  2.06 us (2%)
    pallas_call x1, Pallas kernels, local(): call(fields, wind_east, wind_north, owner, counts, w_in, w_two, w_three,...  102 us

profile of v5, /device:TPU:32, one launch (start us, length us, event | category | flops | bytes accessed | tf_op | source)
XLA Modules:
  0.0 104.1 jit_solution(15603846901867639809)
XLA Ops:
  0.0 102.1 %coupled_steps.1 = f32[32,16,320]{2,1,0:T(8,128)} custom-call(f32[32,16,320]{2,1,0:T(8,128)} %fields.1, f32[32,16,64]{2,1,0:T(8,128)} %wind_east.1, f32[32,16,64]{2,1,0:T(8,128)} %wind_north.1, s32[1,4]{1,0:T(1,128)} %owner.1, s32[1,4]{1,0:T(1,128)} %counts.1, bf16[1,320,512]{2,1,0:T(8,128)(2,1)} %w_in.1, bf16[1,512,512]{2,1,0:T(8,128)(2,1)} %w_two.1, ...), custom_call_target="tpu_custom_call" | custom-call | tf_op jit(solution)/shard_map/coupled_steps/pallas_call | solution.py:703
  102.1 2.1 %copy.11 = f32[32,16,320]{2,1,0:T(8,128)} copy(f32[32,16,320]{2,1,0:T(8,128)} %coupled_steps.1) | data formatting | bytes 1310720

commit v6 on v5

--- a/solution.py
+++ b/solution.py
@@ -498,9 +498,11 @@
 
     for step in range(STEPS):
         if step:
+            copies = halo_copies(step)
+            for copy in copies[:2]:
+                copy.start()
             stage_halo(step)
-            copies = halo_copies(step)
-            for copy in copies:
+            for copy in copies[2:]:
                 copy.start()
             for copy in copies:
                 copy.wait_recv()
@@ -526,7 +528,7 @@
                 cur_bf[slot, :, pl.ds(lo, 128)] = new.astype(BF16)
             return carry
 
-        lax.fori_loop(2, ROWS + 2, sweep_two, 0, unroll=2)
+        lax.fori_loop(2, ROWS + 2, sweep_two, 0, unroll=4)
 
         for cls in range(2):
             cells = cur_bf[pl.ds(cls * 16, 16)].reshape(HALF, 384)
@@ -551,16 +553,25 @@
             row = lax.broadcasted_iota(jnp.int32, (count, 1), 0) % pairs
             inside = rank + (row // BLKS * BLKS).astype(F32)
             tail_place = scheme[:, :1] * pairs + inside
-            picked = jnp.where(from_i.astype(F32) == tail_place, 1.0, 0.0)
-            tail_perm_t[...] = picked.astype(BF16)
-            tail_perm[...] = picked.T.astype(BF16)
             place = (scheme[:, :1] * msg + inside).reshape(n_lon, pairs, 1)
             place = jnp.concatenate([place, place + pairs], axis=1).reshape(n_lon * msg, 1)
+
+            def ordered(column, size):
+                row = jnp.broadcast_to(column, (size, 128)).T[:1]
+                to_i, _ = iota(size, size)
+                return one_hot(to_i.astype(F32) == row)
+
+            tail_perm[...] = ordered(tail_place, count)
+            perm[...] = ordered(place, n_lon * msg)
+
+        arrived(step, 0, recv_one, n_lon, 0)
+        reorder(step, 1, recv_one, send_two, recv_two, perm, tail_perm)
+
+        if step == 0:
+            _, from_i = iota(n_lon * pairs, n_lon * pairs)
+            tail_perm_t[...] = one_hot(from_i.astype(F32) == tail_place)
             _, from_i = iota(n_lon * msg, n_lon * msg)
-            picked = jnp.where(from_i.astype(F32) == place, 1.0, 0.0)
-            perm_t[...] = picked.astype(BF16)
-            perm[...] = picked.T.astype(BF16)
-
+            perm_t[...] = one_hot(from_i.astype(F32) == place)
             for load in loads[3:]:
                 load.wait()
             tail_first[...] = jnp.zeros_like(tail_first)
@@ -569,9 +580,6 @@
                 where = (pl.ds(at * TAIL, TAIL), pl.ds(at * HID, HID))
                 tail_first[where] = v_in[0, pl.ds(MAIN, TAIL), :]
                 tail_last[where] = v_out[0, pl.ds(MAIN, TAIL), :]
-
-        arrived(step, 0, recv_one, n_lon, 0)
-        reorder(step, 1, recv_one, send_two, recv_two, perm, tail_perm)
 
         def physics(cls, carry):
             arrived(step, 1, recv_two, n_lon // 2, cls)
@@ -617,12 +625,13 @@
                             x[step + 1, j + 2, pl.ds(0, WIDE), lanes] += added
                         else:
                             result[j, :, lanes] += added
+                if step + 1 == STEPS:
+                    some = pl.ds(8 * blk + 4 * cls, 4)
+                    pltpu.make_async_copy(result.at[some], out.at[some], out_sem.at[0]).start()
             return carry
 
         lax.fori_loop(0, 2, add_home, 0)
 
-    finish = pltpu.make_async_copy(result, out, out_sem.at[0])
-    finish.start()
     for copy in winds:
         copy.wait_send()
     for step in range(STEPS):
@@ -633,7 +642,7 @@
             pltpu.make_async_copy(sent, sent, ex_send.at[step, phase]).wait()
     sent = owner_in.at[pl.ds(0, n_lon - 1)]
     pltpu.make_async_copy(sent, sent, own_send.at[0]).wait()
-    finish.wait()
+    pltpu.make_async_copy(result, out, out_sem.at[0]).wait()
 
 
 def solution(mesh):

time: 104 us -> 102 us (0.981)
  Pallas kernels: 102 us -> 100 us
    pallas_call x1, Pallas kernels: 102 us -> 100 us  [local(): call(fields, wind_east, wind_north, owner, counts, w_in, w_two, w_three,...]
where the time goes in v6:
time: 102 us
  Pallas kernels  100 us (98%)
  local copies, waits for them, and re-layouts  2.06 us (2%)
    pallas_call x1, Pallas kernels, local(): call(fields, wind_east, wind_north, owner, counts, w_in, w_two, w_three,...  100 us
    unnamed x1, local copies, waits for them, and re-layouts  2.06 us

profile of v6, /device:TPU:32, one launch (start us, length us, event | category | flops | bytes accessed | tf_op | source)
XLA Modules:
  0.0 102.3 jit_solution(12423451113041486213)
XLA Ops:
  0.0 100.2 %coupled_steps.1 = f32[32,16,320]{2,1,0:T(8,128)} custom-call(f32[32,16,320]{2,1,0:T(8,128)} %fields.1, f32[32,16,64]{2,1,0:T(8,128)} %wind_east.1, f32[32,16,64]{2,1,0:T(8,128)} %wind_north.1, s32[1,4]{1,0:T(1,128)} %owner.1, s32[1,4]{1,0:T(1,128)} %counts.1, bf16[1,320,512]{2,1,0:T(8,128)(2,1)} %w_in.1, bf16[1,512,512]{2,1,0:T(8,128)(2,1)} %w_two.1, ...), custom_call_target="tpu_custom_call" | custom-call | tf_op jit(solution)/shard_map/coupled_steps/pallas_call | solution.py:712
  100.2 2.1 %copy.11 = f32[32,16,320]{2,1,0:T(8,128)} copy(f32[32,16,320]{2,1,0:T(8,128)} %coupled_steps.1) | data formatting | bytes 1310720

commit v7 on v6

--- a/solution.py
+++ b/solution.py
@@ -23,7 +23,9 @@
 EXT_R = ROWS + 4
 EXT_C = 24
 CELLS = ROWS * WIDE
-HALF = CELLS // 2
+CLASSES = 2
+PART = CELLS // CLASSES
+BAND = 8 // CLASSES
 MAIN = 256
 TILES = ((0, 128), (128, 256), (256, 320))
 TAIL = FEAT - MAIN
@@ -97,7 +99,7 @@
     out_sem,
 ):
     near = n_lon // GROUPS
-    half = near // 2
+    half = near // CLASSES
     piece = COLS // n_lon
     msg = BLKS * piece
     pairs = msg // 2
@@ -112,10 +114,10 @@
     corners = ((south, west), (south, east), (north, west), (north, east))
 
     def class_of(y, z):
-        return (y + z + me_lat) % 2
+        return (y + z + me_lat) % CLASSES
 
     def slot_of(y, z):
-        return y * near + class_of(y, z) * half + z // 2
+        return y * near + class_of(y, z) * half + z // CLASSES
 
     my_class = class_of(my_y, my_z)
     my_slot = slot_of(my_y, my_z)
@@ -125,8 +127,7 @@
 
     row_order = sorted(range(GROUPS), key=lambda step: -hops(step, GROUPS))
     all_steps = sorted(range(near), key=lambda step: -hops(step, near))
-    even_steps = [step for step in all_steps if step % 2 == 0]
-    odd_steps = [step for step in all_steps if step % 2]
+    class_steps = [[step for step in all_steps if step % CLASSES == c] for c in range(CLASSES)]
 
     loads = [
         pltpu.make_async_copy(wind_east, raw_east, load_sem.at[0]),
@@ -326,24 +327,25 @@
     pltpu.make_async_copy(owner_out, owner_in.at[my_slot], own_recv.at[0]).start()
 
     def main_row(cell):
-        blk, at = cell // (HALF // BLKS), cell % (HALF // BLKS)
+        blk, at = cell // (PART // BLKS), cell % (PART // BLKS)
         return at // piece * msg + at % piece * BLKS + blk
 
     def pair_row(cell):
-        blk, at = cell // (HALF // BLKS), cell % (HALF // BLKS)
+        blk, at = cell // (PART // BLKS), cell % (PART // BLKS)
         return at // piece * pairs + at % (piece // 2) * BLKS + blk
 
     def upper(cell):
         return cell % piece >= piece // 2
 
-    to_i, from_i = iota(HALF, HALF)
+    to_i, from_i = iota(PART, PART)
     shuffle = one_hot(to_i == main_row(from_i))
     unshuffle = one_hot(main_row(to_i) == from_i)
-    to_i, from_i = iota(HALF // 2, HALF)
+    to_i, from_i = iota(PART // 2, PART)
     pair_low = one_hot((to_i == pair_row(from_i)) & ~upper(from_i))
     pair_high = one_hot((to_i == pair_row(from_i)) & upper(from_i))
-    to_i, from_i = iota(HALF, HALF // 2)
+    to_i, from_i = iota(PART, PART // 2)
     unpair = one_hot(pair_row(to_i) == from_i)
+    to_i, from_i = iota(PART, 128)
     is_upper = upper(to_i)
     in_low = from_i < TAIL
 
@@ -437,10 +439,13 @@
     def send_class(step, phase, send, recv, cls):
         def one_row(turn, carry):
             y = row_at(turn)
-            odd = (y + my_y + cls + my_class) % 2
-            for even_step, odd_step in zip(even_steps, odd_steps):
-                z = lax.rem(my_z + jnp.where(odd == 1, odd_step, even_step), near)
-                send_to(step, phase, send, recv, 0, y, z, even_step == 0)
+            turn_of = (cls + my_y + 2 * CLASSES - my_class - y + GROUPS * CLASSES) % CLASSES
+            for steps in zip(*class_steps):
+                z_step = steps[0]
+                for at, value in enumerate(steps[1:]):
+                    z_step = jnp.where(turn_of == at + 1, value, z_step)
+                z = lax.rem(my_z + z_step, near)
+                send_to(step, phase, send, recv, 0, y, z, 0 in steps)
             return carry
 
         lax.fori_loop(0, GROUPS, one_row, 0)
@@ -515,28 +520,33 @@
 
         lax.fori_loop(1, EXT_R - 1, sweep_one, 0, unroll=2)
 
-        def sweep_two(r, carry):
-            j = r - 2
-            slot = (j % 8 // 4) * 16 + (j // 8) * 4 + j % 4
-            for (lo, hi), new in zip(TILES, advected(z, r, WIDE)):
+        def sweep_two(cls, t):
+            j = t // BAND * 8 + cls * BAND + t % BAND
+            for (lo, hi), new in zip(TILES, advected(z, j + 2, WIDE)):
                 if step + 1 < STEPS:
-                    x[step + 1, r, pl.ds(0, WIDE), pl.ds(lo, hi - lo)] = new
+                    x[step + 1, j + 2, pl.ds(0, WIDE), pl.ds(lo, hi - lo)] = new
                 else:
                     result[j, :, pl.ds(lo, hi - lo)] = new
                 if hi == FEAT:
                     new = jnp.concatenate([new, new], axis=1)
-                cur_bf[slot, :, pl.ds(lo, 128)] = new.astype(BF16)
-            return carry
-
-        lax.fori_loop(2, ROWS + 2, sweep_two, 0, unroll=4)
-
-        for cls in range(2):
-            cells = cur_bf[pl.ds(cls * 16, 16)].reshape(HALF, 384)
+                cur_bf[cls * (ROWS // CLASSES) + t, :, pl.ds(lo, 128)] = new.astype(BF16)
+
+        def spread(cls, carry):
+            def sweep_some(t, carry):
+                for at in range(4):
+                    sweep_two(cls, 4 * t + at)
+                return carry
+
+            lax.fori_loop(0, ROWS // CLASSES // 4, sweep_some, 0)
+            cells = cur_bf[pl.ds(cls * (ROWS // CLASSES), ROWS // CLASSES)].reshape(PART, 384)
             tails = cells[:, MAIN:]
             moved = dot(shuffle, cells[:, :MAIN])
-            moved_pair = jnp.where(in_low[: HALF // 2], dot(pair_low, tails), dot(pair_high, tails))
+            moved_pair = jnp.where(in_low[: PART // 2], dot(pair_low, tails), dot(pair_high, tails))
             put_class(send_one, step, cls, moved, moved_pair)
             send_class(step, 0, send_one, recv_one, cls)
+            return carry
+
+        lax.fori_loop(0, CLASSES, spread, 0)
 
         if step == 0:
             pltpu.make_async_copy(owner_in, owner_in, own_recv.at[0]).wait()
@@ -582,39 +592,39 @@
                 tail_last[where] = v_out[0, pl.ds(MAIN, TAIL), :]
 
         def physics(cls, carry):
-            arrived(step, 1, recv_two, n_lon // 2, cls)
+            arrived(step, 1, recv_two, n_lon // CLASSES, cls)
             main, pair = class_of_buf(recv_two, step, cls)
             hidden = dot(main, v_in[0, pl.ds(0, MAIN), :])
             extra = dot(pair, tail_first[...])
-            extra = extra.reshape(n_lon // 2, pairs, 2 * HID)
+            extra = extra.reshape(n_lon // CLASSES, pairs, 2 * HID)
             extra = jnp.concatenate([extra[:, :, :HID], extra[:, :, HID:]], axis=1)
-            hidden = silu(hidden + extra.reshape(HALF, HID)).astype(BF16)
+            hidden = silu(hidden + extra.reshape(PART, HID)).astype(BF16)
             hidden = silu(dot(hidden, v_two[0])).astype(BF16)
             hidden = silu(dot(hidden, v_three[0]))
             tendency = dot_t(hidden.astype(BF16), v_out[0, pl.ds(0, MAIN), :])
-            hidden = hidden.reshape(n_lon // 2, msg, HID)
+            hidden = hidden.reshape(n_lon // CLASSES, msg, HID)
             both_cells = jnp.concatenate([hidden[:, :pairs], hidden[:, pairs:]], axis=2)
-            both_cells = both_cells.reshape(HALF // 2, 2 * HID).astype(BF16)
+            both_cells = both_cells.reshape(PART // 2, 2 * HID).astype(BF16)
             put_class(send_three, step, cls, tendency, dot_t(both_cells, tail_last[...]))
             send_class(step, 2, send_three, recv_three, cls)
             return carry
 
-        lax.fori_loop(0, 2, physics, 0)
+        lax.fori_loop(0, CLASSES, physics, 0)
 
         arrived(step, 2, recv_three, n_lon, 0)
         reorder(step, 3, recv_three, send_four, recv_four, perm_t, tail_perm_t)
 
         def add_home(cls, carry):
-            arrived(step, 3, recv_four, n_lon // 2, cls)
+            arrived(step, 3, recv_four, n_lon // CLASSES, cls)
             main, pair = class_of_buf(recv_four, step, cls)
             home = dot(unshuffle, main)
             tail = dot(unpair, pair)
             tail = jnp.where(is_upper, pltpu.roll(tail, TAIL, axis=1), tail)
             for blk in range(BLKS):
-                for r in range(4):
-                    j = 8 * blk + 4 * cls + r
-                    lo = (4 * blk + r) * WIDE
-                    first_cell = (4 * cls + r) * WIDE
+                for r in range(BAND):
+                    j = 8 * blk + BAND * cls + r
+                    lo = (BAND * blk + r) * WIDE
+                    first_cell = (BAND * cls + r) * WIDE
                     for at, hi in ((0, MAIN), (MAIN, FEAT)):
                         part = home if at == 0 else tail[:, :TAIL]
                         part = part[lo : lo + WIDE]
@@ -626,11 +636,11 @@
                         else:
                             result[j, :, lanes] += added
                 if step + 1 == STEPS:
-                    some = pl.ds(8 * blk + 4 * cls, 4)
+                    some = pl.ds(8 * blk + BAND * cls, BAND)
                     pltpu.make_async_copy(result.at[some], out.at[some], out_sem.at[0]).start()
             return carry
 
-        lax.fori_loop(0, 2, add_home, 0)
+        lax.fori_loop(0, CLASSES, add_home, 0)
 
     for copy in winds:
         copy.wait_send()
@@ -674,8 +684,8 @@
         vmem((n_lon, msg // 2, 128), F32),
         vmem((CELLS, CELLS), BF16),
         vmem((CELLS, CELLS), BF16),
-        vmem((HALF, HALF), BF16),
-        vmem((HALF, HALF), BF16),
+        vmem((CELLS // 2, CELLS // 2), BF16),
+        vmem((CELLS // 2, CELLS // 2), BF16),
         vmem((ROWS, WIDE, FEAT), F32),
         vmem((1, FEAT, HID), BF16),
         vmem((1, HID, HID), BF16),
@@ -691,7 +701,7 @@
         dma((1,)),
         dma((1,)),
         dma((STEPS, 4)),
-        dma((STEPS, 4, 2)),
+        dma((STEPS, 4, CLASSES)),
         dma((1,)),
     ]
 

time: 102 us -> 101 us (level); the launches traced: 102 us -> 99.1 us
  Pallas kernels: 100 us -> 97 us
    pallas_call x1, Pallas kernels: 100 us -> 97 us  [local(): call(fields, wind_east, wind_north, owner, counts, w_in, w_two, w_three,...]
where the time goes in v7:
time: 101 us; the launch traced here: 99.1 us
  Pallas kernels  97 us (96%)
  local copies, waits for them, and re-layouts  2.06 us (2%)
    pallas_call x1, Pallas kernels, local(): call(fields, wind_east, wind_north, owner, counts, w_in, w_two, w_three,...  97 us
    unnamed x1, local copies, waits for them, and re-layouts  2.06 us

profile of v7, /device:TPU:32, one launch (start us, length us, event | category | flops | bytes accessed | tf_op | source)
XLA Modules:
  0.0 99.1 jit_solution(2018550118224206189)
XLA Ops:
  0.0 97.0 %coupled_steps.1 = f32[32,16,320]{2,1,0:T(8,128)} custom-call(f32[32,16,320]{2,1,0:T(8,128)} %fields.1, f32[32,16,64]{2,1,0:T(8,128)} %wind_east.1, f32[32,16,64]{2,1,0:T(8,128)} %wind_north.1, s32[1,4]{1,0:T(1,128)} %owner.1, s32[1,4]{1,0:T(1,128)} %counts.1, bf16[1,320,512]{2,1,0:T(8,128)(2,1)} %w_in.1, bf16[1,512,512]{2,1,0:T(8,128)(2,1)} %w_two.1, ...), custom_call_target="tpu_custom_call" | custom-call | tf_op jit(solution)/shard_map/coupled_steps/pallas_call | solution.py:722
  97.0 2.1 %copy.11 = f32[32,16,320]{2,1,0:T(8,128)} copy(f32[32,16,320]{2,1,0:T(8,128)} %coupled_steps.1) | data formatting | bytes 1310720

commit v8 on v7

--- a/solution.py
+++ b/solution.py
@@ -140,7 +140,7 @@
         pltpu.make_async_copy(w_three, v_three, load_sem.at[5]),
         pltpu.make_async_copy(w_out, v_out, load_sem.at[6]),
     ]
-    for load in loads:
+    for load in loads[:3]:
         load.start()
 
     barrier = pltpu.get_barrier_semaphore()
@@ -317,6 +317,8 @@
     first = halo_copies(0)
     for copy in winds + first:
         copy.start()
+    for load in loads[3:]:
+        load.start()
 
     def tell_owner(step, carry):
         there = lax.rem(me + step, n_lon)

time: 101 us -> 101 us (level); the launches traced: 99.1 us -> 101 us
  Pallas kernels: 97 us -> 98.6 us
    pallas_call x1, Pallas kernels: 97 us -> 98.6 us  [local(): call(fields, wind_east, wind_north, owner, counts, w_in, w_two, w_three,...]
where the time goes in v8:
time: 101 us
  Pallas kernels  98.6 us (98%)
  local copies, waits for them, and re-layouts  2.06 us (2%)
    pallas_call x1, Pallas kernels, local(): call(fields, wind_east, wind_north, owner, counts, w_in, w_two, w_three,...  98.6 us
    unnamed x1, local copies, waits for them, and re-layouts  2.06 us

profile of v8, /device:TPU:32, one launch (start us, length us, event | category | flops | bytes accessed | tf_op | source)
XLA Modules:
  0.0 100.6 jit_solution(2899778105227885402)
XLA Ops:
  0.0 98.6 %coupled_steps.1 = f32[32,16,320]{2,1,0:T(8,128)} custom-call(f32[32,16,320]{2,1,0:T(8,128)} %fields.1, f32[32,16,64]{2,1,0:T(8,128)} %wind_east.1, f32[32,16,64]{2,1,0:T(8,128)} %wind_north.1, s32[1,4]{1,0:T(1,128)} %owner.1, s32[1,4]{1,0:T(1,128)} %counts.1, bf16[1,320,512]{2,1,0:T(8,128)(2,1)} %w_in.1, bf16[1,512,512]{2,1,0:T(8,128)(2,1)} %w_two.1, ...), custom_call_target="tpu_custom_call" | custom-call | tf_op jit(solution)/shard_map/coupled_steps/pallas_call | solution.py:724
  98.6 2.1 %copy.11 = f32[32,16,320]{2,1,0:T(8,128)} copy(f32[32,16,320]{2,1,0:T(8,128)} %coupled_steps.1) | data formatting | bytes 1310720
